TPU v7x, 128 devices: a whole 4x4x4 slice. The times are simulated.
128 devices in a mesh: seq: 16 (over y_lo, x, core), ch: 8 (over z, y_hi).
Axes of the slice: x: 4, y: 4 (y_hi: 2, y_lo: 2; y = y_hi * 2 + y_lo), z: 4, core: 2. Of those that a mesh axis runs over, the one named last changes fastest.
Arguments:
- gate_input: bfloat16 [2048, 8192], P('seq', 'ch'), may hold values from -6 to 6
- value_input: bfloat16 [2048, 8192], P('seq', 'ch'), may hold values from -6 to 6
- filter_taps: float32 [2048, 8192], P('seq', 'ch'), may hold values from -1.5 to 1.5
- out_weight: bfloat16 [8192, 8192], P('ch'), may hold values from -0.0625 to 0.0625
- grad_output: bfloat16 [2048, 8192], P('seq', 'ch'), may hold values from -6 to 6
Outputs:
- block_output: bfloat16 [2048, 8192], P('seq', 'ch')
- gate_grad: bfloat16 [2048, 8192], P('seq', 'ch')
- value_grad: bfloat16 [2048, 8192], P('seq', 'ch')
- filter_grad: float32 [2048, 8192], P('seq', 'ch')
- weight_grad: bfloat16 [8192, 8192], P('ch', 'seq')
All inputs are finite; a program needn't handle non-finite values.
Results may differ from a plain program's by a relative error of at most 0.017.
Values may be sent and summed in bfloat16 or wider, within the bound.
No kernel may reach another device: no remote copies, remote signals or barrier semaphores. Data moves between devices by JAX's collectives and lax.ppermute only.
A program may use at most 128 MiB of HBM per device.

v0:
```python
import functools
import math

import jax
import jax.numpy as jnp
import numpy as np
from jax import lax
from jax.experimental import pallas as pl
from jax.experimental.pallas import tpu as pltpu
from jax.sharding import PartitionSpec as P

BLOCKS = 16
INNER = 128
PERIOD = 2 * BLOCKS * INNER
HALF = 64
GROUP = 16
BF16 = jnp.bfloat16
F32 = jnp.float32


def plane_order():
    order = [(0, False), (BLOCKS, False)]
    for freq in range(1, BLOCKS):
        order += [(freq, False), (freq, True)]
    return order


def outer_matrices():
    blocks = np.arange(BLOCKS)
    forward = np.zeros((2 * BLOCKS, BLOCKS))
    inverse = np.zeros((BLOCKS, 2 * BLOCKS))
    for plane, (freq, imaginary) in enumerate(plane_order()):
        turn = 2.0 * np.pi * ((freq * blocks) % (2 * BLOCKS)) / (2 * BLOCKS)
        weight = (1.0 if freq in (0, BLOCKS) else 2.0) / PERIOD
        wave = -np.sin(turn) if imaginary else np.cos(turn)
        forward[plane] = wave
        inverse[:, plane] = weight * wave
    eye = np.eye(GROUP)
    return np.kron(forward, eye), np.kron(inverse, eye)


def inner_matrices():
    freqs = np.arange(BLOCKS + 1)[:, None, None] + 2 * BLOCKS * np.arange(INNER)[None, :, None]
    turn = 2.0 * np.pi * ((freqs * np.arange(INNER)[None, None, :]) % PERIOD) / PERIOD
    cos, sin = np.cos(turn), np.sin(turn)
    top = np.concatenate([cos, sin], axis=2)
    bottom = np.concatenate([-sin, cos], axis=2)
    forward = np.concatenate([top, bottom], axis=1)
    return forward, np.swapaxes(forward, 1, 2)


def dot(left, right):
    return jnp.dot(left, right, preferred_element_type=F32)


def lane_low(shape):
    return lax.broadcasted_iota(jnp.int32, shape, len(shape) - 1) < HALF


def swap(array):
    return pltpu.roll(array, HALF, array.ndim - 1)


def pack_kernel(value_ref, taps_ref, out_ref):
    for pair in range(value_ref.shape[1] // INNER):
        lanes = pl.ds(pair * INNER, INNER)
        value = value_ref[:, lanes].astype(F32)
        taps = taps_ref[:, lanes]
        low = lane_low(value.shape)
        out_ref[2 * pair] = jnp.where(low, value, swap(taps)).astype(BF16)
        out_ref[2 * pair + 1] = jnp.where(low, swap(value), taps).astype(BF16)


def outer_forward(read_group, outer_ref, planes_ref):
    for group in range(INNER // GROUP):
        rows = pl.ds(group * GROUP, GROUP)
        block = read_group(rows).reshape(BLOCKS * GROUP, INNER)
        wide = dot(outer_ref[...], block).astype(BF16)
        planes_ref[:, rows, :] = wide.reshape(2 * BLOCKS, GROUP, INNER)


def inner_forward(freq, inner_ref, planes_ref):
    if freq in (0, BLOCKS):
        return dot(inner_ref[freq, :, :INNER], planes_ref[0 if freq == 0 else 1])
    pair = planes_ref[2 * freq : 2 * freq + 2].reshape(2 * INNER, INNER)
    return dot(inner_ref[freq], pair)


def inner_inverse(freq, product, inner_ref, planes_ref):
    if freq in (0, BLOCKS):
        planes_ref[0 if freq == 0 else 1] = dot(inner_ref[freq, :INNER, :], product).astype(BF16)
    else:
        back = dot(inner_ref[freq], product).astype(BF16)
        planes_ref[2 * freq : 2 * freq + 2] = back.reshape(2, INNER, INNER)


def outer_inverse(group, outer_ref, planes_ref):
    planes = planes_ref[:, pl.ds(group * GROUP, GROUP), :].reshape(2 * BLOCKS * GROUP, INNER)
    return dot(outer_ref[...], planes).reshape(BLOCKS, GROUP, INNER)


def convolve_kernel(pair_ref, outer_ref, inner_ref, inner_back_ref, outer_back_ref, out_ref, spec_ref, planes_ref, back_ref):
    outer_forward(lambda rows: pair_ref[:, rows, :], outer_ref, planes_ref)
    for freq in range(BLOCKS + 1):
        spec = inner_forward(freq, inner_ref, planes_ref)
        spec_ref[freq] = spec.astype(BF16)
        other = swap(spec)
        re, im = spec[:INNER], spec[INNER:]
        other_re, other_im = other[:INNER], other[INNER:]
        product = jnp.concatenate([re * other_re - im * other_im, re * other_im + im * other_re], 0)
        inner_inverse(freq, product.astype(BF16), inner_back_ref, back_ref)
    half_groups = INNER // GROUP // 2
    for group in range(half_groups):
        first = outer_inverse(group, outer_back_ref, back_ref)
        second = outer_inverse(group + half_groups, outer_back_ref, back_ref)
        packed = jnp.where(lane_low(first.shape), first, second)
        out_ref[:, pl.ds(group * GROUP, GROUP), :] = packed.astype(BF16)


def correlate_kernel(grad_ref, spec_ref, outer_ref, inner_ref, inner_back_ref, outer_back_ref, out_ref, wide_ref, planes_ref, back_ref):
    for block in range(BLOCKS):
        packed = grad_ref[block].astype(F32)
        turned = swap(packed)
        low = lane_low(packed.shape)
        wide_ref[block, :HALF] = jnp.where(low, packed, turned).astype(BF16)
        wide_ref[block, HALF:] = jnp.where(low, turned, packed).astype(BF16)
    outer_forward(lambda rows: wide_ref[:, rows, :], outer_ref, planes_ref)
    for freq in range(BLOCKS + 1):
        grad = inner_forward(freq, inner_ref, planes_ref)
        spec = spec_ref[freq].astype(F32)
        re, im = spec[:INNER], spec[INNER:]
        grad_re, grad_im = grad[:INNER], grad[INNER:]
        product = jnp.concatenate([re * grad_re + im * grad_im, re * grad_im - im * grad_re], 0)
        inner_inverse(freq, product.astype(BF16), inner_back_ref, back_ref)
    for group in range(INNER // GROUP):
        out_ref[:, pl.ds(group * GROUP, GROUP), :] = outer_inverse(group, outer_back_ref, back_ref).astype(BF16)


def gate_kernel(recv_ref, gate_ref, conv_ref, gated_ref):
    for pair in range(BLOCKS // 2):
        first = recv_ref[2 * pair].astype(F32)
        second = recv_ref[2 * pair + 1].astype(F32)
        low = lane_low(first.shape)
        conv = jnp.concatenate([jnp.where(low, first, swap(second)), jnp.where(low, swap(first), second)], 0)
        lanes = pl.ds(pair * INNER, INNER)
        conv_ref[:, lanes] = conv
        gated_ref[:, lanes] = (gate_ref[:, lanes].astype(F32) * conv).astype(BF16)


def finish_kernel(scale, recv_ref, value_grad_ref, filter_grad_ref):
    for pair in range(BLOCKS // 2):
        first = recv_ref[2 * pair].astype(F32)
        second = recv_ref[2 * pair + 1].astype(F32)
        low = lane_low(first.shape)
        lanes = pl.ds(pair * INNER, INNER)
        filter_grad_ref[:, lanes] = jnp.where(low, first, swap(second)) * scale
        value_grad_ref[:, lanes] = jnp.where(low, swap(first), second).astype(BF16)


def pre_grad_kernel(grad_ref, weight_ref, gate_ref, pre_ref, cotangent_ref, columns_ref):
    step = pl.program_id(0)
    grad = grad_ref[0]
    part = lax.dot_general(grad, weight_ref[...], (((1,), (1,)), ((), ())), preferred_element_type=F32)
    width = columns_ref.shape[2]
    for piece in range(columns_ref.shape[0]):
        columns_ref[piece] = grad[:, piece * width : (piece + 1) * width]

    @pl.when(step == 0)
    def _():
        pre_ref[...] = part

    @pl.when(step > 0)
    def _():
        pre_ref[...] += part

    @pl.when(step == pl.num_programs(0) - 1)
    def _():
        for pair in range(BLOCKS // 2):
            lanes = pl.ds(pair * INNER, INNER)
            cotangent = pre_ref[:, lanes] * gate_ref[:, lanes].astype(F32)
            top, bottom = cotangent[:HALF], cotangent[HALF:]
            low = lane_low(top.shape)
            cotangent_ref[2 * pair] = jnp.where(low, top, swap(bottom)).astype(BF16)
            cotangent_ref[2 * pair + 1] = jnp.where(low, swap(top), bottom).astype(BF16)


def project_kernel(gated_ref, weight_ref, out_ref):
    out_ref[0] = dot(gated_ref[...], weight_ref[...]).astype(BF16)


def shape(dims, kind):
    return jax.ShapeDtypeStruct(dims, kind)


def params(mebibytes=48):
    return pltpu.CompilerParams(vmem_limit_bytes=mebibytes * 1024 * 1024)


def exchange(array, axis):
    return lax.all_to_all(array, axis, split_axis=0, concat_axis=0, tiled=True)


def body(gate_input, value_input, filter_taps, out_weight, grad_output):
    rows, channels = gate_input.shape
    shards = lax.axis_size("seq")
    groups = lax.axis_size("ch")
    scale = 1.0 / math.sqrt(rows * shards)
    width = channels * groups // shards
    outer, outer_back = (jnp.asarray(m, BF16) for m in outer_matrices())
    inner, inner_back = (jnp.asarray(m, BF16) for m in inner_matrices())
    planes = pltpu.VMEM((2 * BLOCKS, INNER, INNER), BF16)

    pair = pl.pallas_call(
        pack_kernel, out_shape=shape((shards, rows, INNER), BF16), compiler_params=params(), name="pack_pair"
    )(value_input, filter_taps)
    pair = exchange(pair, "seq")
    grad_full = exchange(jnp.broadcast_to(grad_output[None], (groups, rows, channels)), "ch")

    packed, spec = pl.pallas_call(
        convolve_kernel,
        out_shape=(shape((shards, HALF, INNER), BF16), shape((BLOCKS + 1, 2 * INNER, INNER), BF16)),
        scratch_shapes=[planes, planes],
        compiler_params=params(),
        name="convolve",
    )(pair, outer, inner, inner_back, outer_back)
    conv, gated = pl.pallas_call(
        gate_kernel,
        out_shape=(shape((rows, channels), F32), shape((rows, channels), BF16)),
        compiler_params=params(),
        name="gate",
    )(exchange(packed, "seq"), gate_input)
    gated_all = lax.all_gather(gated, "seq", axis=0, tiled=True)

    whole = lambda *dims: pl.BlockSpec(dims, lambda step: (0,) * len(dims))
    pre_grad, cotangent, columns = pl.pallas_call(
        pre_grad_kernel,
        grid=(groups,),
        in_specs=[
            pl.BlockSpec((1, rows, channels), lambda step: (step, 0, 0)),
            pl.BlockSpec((channels, channels), lambda step: (0, step)),
            whole(rows, channels),
        ],
        out_specs=(
            whole(rows, channels),
            whole(shards, HALF, INNER),
            pl.BlockSpec((shards // groups, rows, width), lambda step: (step, 0, 0)),
        ),
        out_shape=(
            shape((rows, channels), F32),
            shape((shards, HALF, INNER), BF16),
            shape((shards, rows, width), BF16),
        ),
        compiler_params=params(),
        name="pre_grad",
    )(grad_full, out_weight, gate_input)
    gate_grad = (pre_grad * conv).astype(BF16)

    returned = pl.pallas_call(
        correlate_kernel,
        out_shape=shape((shards, rows, INNER), BF16),
        scratch_shapes=[pltpu.VMEM((BLOCKS, INNER, INNER), BF16), planes, planes],
        compiler_params=params(),
        name="correlate",
    )(exchange(cotangent, "seq"), spec, outer, inner, inner_back, outer_back)
    value_grad, filter_grad = pl.pallas_call(
        functools.partial(finish_kernel, scale),
        out_shape=(shape((rows, channels), BF16), shape((rows, channels), F32)),
        compiler_params=params(),
        name="finish",
    )(exchange(returned, "seq"))

    projected = pl.pallas_call(
        project_kernel,
        grid=(groups,),
        in_specs=[whole(rows, channels), pl.BlockSpec((channels, channels), lambda step: (0, step))],
        out_specs=pl.BlockSpec((1, rows, channels), lambda step: (step, 0, 0)),
        out_shape=shape((groups, rows, channels), BF16),
        compiler_params=params(),
        name="project",
    )(gated, out_weight)
    block_output = jnp.sum(exchange(projected, "ch").astype(F32), axis=0).astype(BF16)

    columns = exchange(columns, "seq").reshape(shards * rows, width)
    summed = lax.dot_general(gated_all, columns, (((0,), (0,)), ((), ())), preferred_element_type=F32)
    weight_grad = (summed * scale).astype(BF16)
    return (block_output, gate_grad, value_grad, filter_grad, weight_grad)


def solution(mesh):
    placed = (P("seq", "ch"), P("seq", "ch"), P("seq", "ch"), P("ch", None), P("seq", "ch"))
    return jax.shard_map(
        body,
        mesh=mesh,
        in_specs=placed,
        out_specs=(P("seq", "ch"), P("seq", "ch"), P("seq", "ch"), P("seq", "ch"), P("ch", "seq")),
        check_vma=False,
    )
```

profile of v0, /device:TPU:1, one launch (start us, length us, event | category | flops | bytes accessed | tf_op | source)
XLA Modules:
  0.0 224.3 jit_solution(3330627956209486732)
XLA Ops:
  7.2 0.0 copy-start
  7.2 0.0 all-gather.2.cloned.1.call-start
  7.2 0.0 copy-start.10
  7.2 1.2 copy-done.10
  8.4 0.0 copy-start.15
  8.4 0.9 copy-done.15
  9.4 0.2 pack_pair.1
  9.6 16.5 %all_to_all.35.pair_ref = bf16[16,128,128]{2,1,0:T(8,128)(2,1)S(1)} all-to-all(bf16[16,128,128]{2,1,0:T(8,128)(2,1)S(1)} %pack_pair.1), channel_id=1, replica_groups=mesh['seq'=16,'ch'=8] {'seq'}, dimensions={0} | all-to-all | bytes 1048576 | tf_op jit(solution)/shard_map/all_to_all | solution.py:200
  26.1 0.0 copy-done
  26.1 0.0 copy-start.6
  26.1 0.9 copy-done.6
  27.0 0.0 copy-start.8
  27.0 0.9 copy-done.8
  28.0 0.0 copy-start.2
  28.0 4.4 %convolve.1 = (bf16[16,64,128]{2,1,0:T(8,128)(2,1)S(1)}, bf16[17,256,128]{2,1,0:T(8,128)(2,1)S(1)}) custom-call(bf16[16,128,128]{2,1,0:T(8,128)(2,1)S(1)} %all_to_all.35.pair_ref, bf16[512,256]{1,0:T(8,128)(2,1)S(1)} %copy-done.6, bf16[17,256,256]{2,1,0:T(8,128)(2,1)S(1)} %copy-done, bf16[17,256,256]{2,1,0:T(8,128)(2,1)} %constant.16.clone.inner_back_ref, ...), custom_call_target="tpu_custom_call" | custom-call | tf_op jit(solution)/shard_map/convolve/pallas_call | solution.py:219
  32.4 10.7 %all_to_all.36.recv_ref = bf16[16,64,128]{2,1,0:T(8,128)(2,1)S(1)} all-to-all(bf16[16,64,128]{2,1,0:T(8,128)(2,1)S(1)} %get-tuple-element.14), channel_id=1, replica_groups=mesh['seq'=16,'ch'=8] {'seq'}, dimensions={0} | all-to-all | bytes 524288 | tf_op jit(solution)/shard_map/all_to_all | solution.py:200
  43.1 0.0 copy-done.2
  43.1 0.2 gate.1
  43.3 0.0 copy-start.4
  43.3 0.7 copy-done.4
  44.0 0.0 copy-start.11
  44.0 0.8 copy-done.11
  44.8 0.0 all-gather.2.cloned.1.call-update
  44.8 1.2 broadcast_in_dim.2
  46.0 0.0 copy-start.3
  46.1 55.3 %all_to_all.37.grad_ref = bf16[8,128,1024]{2,1,0:T(8,128)(2,1)S(1)} all-to-all(bf16[8,128,1024]{2,1,0:T(8,128)(2,1)S(1)} %broadcast_in_dim.2), channel_id=1, replica_groups=mesh['seq'=16,'ch'=8] {'ch'}, dimensions={0} | all-to-all | bytes 4194304 | tf_op jit(solution)/shard_map/all_to_all | solution.py:200
  101.4 0.0 copy-done.3
  101.4 0.0 copy-start.7
  101.4 0.0 copy-start.9
  101.4 11.4 %pre_grad.1 = (f32[128,1024]{1,0:T(8,128)S(1)}, bf16[16,64,128]{2,1,0:T(8,128)(2,1)S(1)}, bf16[16,128,512]{2,1,0:T(8,128)(2,1)S(1)}) custom-call(bf16[8,128,1024]{2,1,0:T(8,128)(2,1)S(1)} %all_to_all.37.grad_ref, bf16[1024,8192]{1,0:T(8,128)(2,1)} %weight_ref.3, bf16[128,1024]{1,0:T(8,128)(2,1)S(1)} %copy-done.3), custom_call_target="tpu_custom_call" | custom-call | tf_op jit(solution)/shard_map/pre_grad/pallas_call | solution.py:235
  112.7 0.0 copy-start.1
  112.8 1.3 copy-done.1
  114.1 0.0 copy-start.13
  114.1 0.8 copy-done.13
  114.9 10.9 %all_to_all.38.grad_ref = bf16[16,64,128]{2,1,0:T(8,128)(2,1)S(1)} all-to-all(bf16[16,64,128]{2,1,0:T(8,128)(2,1)S(1)} %get-tuple-element.18), channel_id=1, replica_groups=mesh['seq'=16,'ch'=8] {'seq'}, dimensions={0} | all-to-all | bytes 524288 | tf_op jit(solution)/shard_map/all_to_all | solution.py:200
  125.7 0.0 copy-done.7
  125.7 0.0 copy-done.9
  125.7 5.2 %correlate.1 = bf16[16,128,128]{2,1,0:T(8,128)(2,1)} custom-call(bf16[16,64,128]{2,1,0:T(8,128)(2,1)S(1)} %all_to_all.38.grad_ref, bf16[17,256,128]{2,1,0:T(8,128)(2,1)S(1)} %get-tuple-element.19.spec_ref, bf16[512,256]{1,0:T(8,128)(2,1)S(1)} %copy-done.7, bf16[17,256,256]{2,1,0:T(8,128)(2,1)S(1)} %copy-done, ...), custom_call_target="tpu_custom_call" | custom-call | tf_op jit(solution)/shard_map/correlate/pallas_call | solution.py:258
  130.9 4.2 %all-to-all-start.5 = ((bf16[16,128,128]{2,1,0:T(8,128)(2,1)}), bf16[16,128,128]{2,1,0:T(8,128)(2,1)S(1)}, u32[]{:S(2)}, u32[]{:S(2)}) async-start(bf16[16,128,128]{2,1,0:T(8,128)(2,1)} %correlate.1), calls=%async_computation.5 | async-start | bytes 1048576 | tf_op jit(solution)/shard_map/all_to_all | solution.py:200
  135.1 0.0 copy-start.5
  135.1 0.9 copy-done.5
  136.1 9.3 %project.1 = bf16[8,128,1024]{2,1,0:T(8,128)(2,1)S(1)} custom-call(bf16[128,1024]{1,0:T(8,128)(2,1)S(1)} %copy-done.5, bf16[1024,8192]{1,0:T(8,128)(2,1)} %weight_ref.3), custom_call_target="tpu_custom_call" | custom-call | tf_op jit(solution)/shard_map/project/pallas_call | solution.py:272
  145.4 0.0 all-to-all-done.5.recv_ref
  145.4 30.6 %all_to_all.39 = bf16[8,128,1024]{2,1,0:T(8,128)(2,1)} all-to-all(bf16[8,128,1024]{2,1,0:T(8,128)(2,1)S(1)} %project.1), channel_id=1, replica_groups=mesh['seq'=16,'ch'=8] {'ch'}, dimensions={0} | all-to-all | bytes 4194304 | tf_op jit(solution)/shard_map/all_to_all | solution.py:200
  176.0 0.0 copy-start.12
  176.0 0.0 copy-start.14
  176.0 7.5 %all-to-all-start.6 = ((bf16[16,128,512]{2,1,0:T(8,128)(2,1)}), bf16[16,128,512]{2,1,0:T(8,128)(2,1)}, u32[]{:S(2)}, u32[]{:S(2)}) async-start(bf16[16,128,512]{2,1,0:T(8,128)(2,1)} %copy-done.1), calls=%async_computation.6 | async-start | bytes 4194304 | tf_op jit(solution)/shard_map/all_to_all | solution.py:200
  183.5 0.0 copy-done.12
  183.5 0.0 copy-done.14
  183.5 0.8 multiply_convert_fusion.1
  184.3 1.1 finish.1
  185.4 2.7 %reduce_sum.12 = bf16[128,1024]{1,0:T(8,128)(2,1)} reduce(bf16[8,128,1024]{2,1,0:T(8,128)(2,1)} %all_to_all.39, bf16[]{:T(256)} %constant.5.clone.1), dimensions={0}, to_apply=%region_0.0 | reduce | flops 917504 | bytes 2359298 | tf_op jit(solution)/shard_map/reduce_sum | solution.py:281
  188.1 23.1 %all-to-all-done.6 = bf16[16,128,512]{2,1,0:T(8,128)(2,1)} async-done(((bf16[16,128,512]{2,1,0:T(8,128)(2,1)}), bf16[16,128,512]{2,1,0:T(8,128)(2,1)}, u32[]{:S(2)}, u32[]{:S(2)}) %all-to-all-start.6) | async-done | bytes 2097184 | tf_op jit(solution)/shard_map/all_to_all | solution.py:200
  211.2 0.0 all-gather.2.cloned.1.call-done
  211.2 6.2 %multiply_convert_fusion = bf16[1024,512]{1,0:T(8,128)(2,1)} fusion(bf16[2048,1024]{1,0:T(8,128)(2,1)} %all-gather.2.cloned.1.call-done, bf16[2048,512]{1,0:T(8,128)(2,1)} %bitcast), kind=kOutput, calls=%fused_computation | convolution fusion | flops 2148532224 | bytes 7340032 | tf_op jit(solution)/shard_map/dot_general | solution.py:284
Async XLA Ops:
  7.2 18.9 %copy-start = (bf16[17,256,256]{2,1,0:T(8,128)(2,1)S(1)}, bf16[17,256,256]{2,1,0:T(8,128)(2,1)}, u32[]{:S(2)}) copy-start(bf16[17,256,256]{2,1,0:T(8,128)(2,1)} %constant.15.clone.inner_ref) | copy-start | bytes 6684676
  7.2 204.0 %all-gather.2.cloned.1.call-start = ((), (), s32[]{:S(2)}) async-start(), calls=%async_computation.7 | async-start | bytes 4456448 | tf_op jit(solution)/shard_map/all_gather | solution.py:232
  7.2 1.2 copy-start.10
  8.4 0.9 copy-start.15
  26.1 1.0 copy-start.6
  27.0 0.9 copy-start.8
  28.0 15.1 %copy-start.2 = (bf16[128,1024]{1,0:T(8,128)(2,1)S(1)}, bf16[128,1024]{1,0:T(8,128)(2,1)}, u32[]{:S(2)}) copy-start(bf16[128,1024]{1,0:T(8,128)(2,1)} %gate_ref.3) | copy-start | bytes 786436
  43.3 0.7 copy-start.4
  44.0 0.8 copy-start.11
  46.0 55.3 %copy-start.3 = (bf16[128,1024]{1,0:T(8,128)(2,1)S(1)}, bf16[128,1024]{1,0:T(8,128)(2,1)}, u32[]{:S(2)}) copy-start(bf16[128,1024]{1,0:T(8,128)(2,1)} %gate_ref.3) | copy-start | bytes 786436
  101.4 24.4 %copy-start.7 = (bf16[512,256]{1,0:T(8,128)(2,1)S(1)}, bf16[512,256]{1,0:T(8,128)(2,1)}, u32[]{:S(2)}) copy-start(bf16[512,256]{1,0:T(8,128)(2,1)} %constant.13.clone.outer_ref) | copy-start | bytes 786436
  101.4 24.4 %copy-start.9 = (bf16[256,512]{1,0:T(8,128)(2,1)S(1)}, bf16[256,512]{1,0:T(8,128)(2,1)}, u32[]{:S(2)}) copy-start(bf16[256,512]{1,0:T(8,128)(2,1)} %constant.14.clone.outer_back_ref) | copy-start | bytes 786436
  112.7 1.3 copy-start.1
  114.1 0.8 copy-start.13
  130.9 14.4 %all-to-all-start.5 = ((bf16[16,128,128]{2,1,0:T(8,128)(2,1)}), bf16[16,128,128]{2,1,0:T(8,128)(2,1)S(1)}, u32[]{:S(2)}, u32[]{:S(2)}) async-start(bf16[16,128,128]{2,1,0:T(8,128)(2,1)} %correlate.1), calls=%async_computation.5 | async-start | bytes 1048576 | tf_op jit(solution)/shard_map/all_to_all | solution.py:200
  135.1 0.9 copy-start.5
  176.0 7.5 %copy-start.12 = (f32[128,1024]{1,0:T(8,128)S(1)}, f32[128,1024]{1,0:T(8,128)}, u32[]{:S(2)}) copy-start(f32[128,1024]{1,0:T(8,128)} %copy-done.11) | copy-start | bytes 1572868
  176.0 7.5 %copy-start.14 = (f32[128,1024]{1,0:T(8,128)S(1)}, f32[128,1024]{1,0:T(8,128)}, u32[]{:S(2)}) copy-start(f32[128,1024]{1,0:T(8,128)} %copy-done.13) | copy-start | bytes 1572868
  176.0 35.2 %all-to-all-start.6 = ((bf16[16,128,512]{2,1,0:T(8,128)(2,1)}), bf16[16,128,512]{2,1,0:T(8,128)(2,1)}, u32[]{:S(2)}, u32[]{:S(2)}) async-start(bf16[16,128,512]{2,1,0:T(8,128)(2,1)} %copy-done.1), calls=%async_computation.6 | async-start | bytes 4194304 | tf_op jit(solution)/shard_map/all_to_all | solution.py:200
Sparse Core Ops, SparseCore 0:
  45.0 52.4 all-gather.1
where the time goes:
time: 225 us; the launch traced here: 224 us
  blocking collectives  124 us (55%)
  Pallas kernels  31.8 us (14%)
  waiting for transfers between devices  23.1 us (10%)
  between operations  14.2 us (6%)
  starting transfers between devices  11.7 us (5%)
  local copies, waits for them, and re-layouts  9.82 us (4%)
  matrix products  6.2 us (3%)
  other arithmetic  3.49 us (2%)
    all_to_all x5, blocking collectives, exchange(): return lax.all_to_all(array, axis, split_axis=0, concat_axis=0, tiled=True)  124 us
    all_to_all x2, waiting for transfers between devices, exchange(): return lax.all_to_all(array, axis, split_axis=0, concat_axis=0, tiled=True)  23.1 us
    all_to_all x2, starting transfers between devices, exchange(): return lax.all_to_all(array, axis, split_axis=0, concat_axis=0, tiled=True)  11.7 us
    pallas_call x1, Pallas kernels, body(): pl.pallas_call(pre_grad_kernel, grid=(groups,), in_specs=[pl.BlockSpec((1...  11.4 us
    pallas_call x1, Pallas kernels, body(): pl.pallas_call(project_kernel, grid=(groups,), in_specs=[whole(rows, chan...  9.31 us
    unnamed x32, local copies, waits for them, and re-layouts  8.61 us
    dot_general x1, matrix products, body(): lax.dot_general(gated_all, columns, (((0,), (0,)), ((), ())), preferred_e...  6.2 us
    pallas_call x1, Pallas kernels, body(): pl.pallas_call(correlate_kernel, out_shape=shape((shards, rows, INNER), B...  5.22 us
  transfers between devices with their start and end apart: 3, of which 1 were waited for; matrix products, arithmetic and copies ran while one was open for 2% of the time, Pallas kernels for 12%

commit v1 on v0

--- a/solution.py
+++ b/solution.py
@@ -157,42 +157,50 @@
         value_grad_ref[:, lanes] = jnp.where(low, swap(first), second).astype(BF16)
 
 
-def pre_grad_kernel(grad_ref, weight_ref, gate_ref, pre_ref, cotangent_ref, columns_ref):
+def pre_grad_kernel(grad_ref, weight_ref, gate_ref, conv_ref, gate_grad_ref, cotangent_ref, total_ref):
     step = pl.program_id(0)
-    grad = grad_ref[0]
-    part = lax.dot_general(grad, weight_ref[...], (((1,), (1,)), ((), ())), preferred_element_type=F32)
-    width = columns_ref.shape[2]
-    for piece in range(columns_ref.shape[0]):
-        columns_ref[piece] = grad[:, piece * width : (piece + 1) * width]
+    width = grad_ref.shape[2]
+    part = 0.0
+    for piece in range(grad_ref.shape[0]):
+        weight = weight_ref[:, piece * width : (piece + 1) * width]
+        part += lax.dot_general(weight, grad_ref[piece], (((1,), (1,)), ((), ())), preferred_element_type=F32)
 
     @pl.when(step == 0)
     def _():
-        pre_ref[...] = part
+        total_ref[...] = part
 
     @pl.when(step > 0)
     def _():
-        pre_ref[...] += part
+        total_ref[...] += part
 
     @pl.when(step == pl.num_programs(0) - 1)
     def _():
         for pair in range(BLOCKS // 2):
             lanes = pl.ds(pair * INNER, INNER)
-            cotangent = pre_ref[:, lanes] * gate_ref[:, lanes].astype(F32)
+            pre = total_ref[lanes, :].T
+            gate_grad_ref[:, lanes] = (pre * conv_ref[:, lanes]).astype(BF16)
+            cotangent = pre * gate_ref[:, lanes].astype(F32)
             top, bottom = cotangent[:HALF], cotangent[HALF:]
             low = lane_low(top.shape)
             cotangent_ref[2 * pair] = jnp.where(low, top, swap(bottom)).astype(BF16)
             cotangent_ref[2 * pair + 1] = jnp.where(low, swap(top), bottom).astype(BF16)
 
 
-def project_kernel(gated_ref, weight_ref, out_ref):
-    out_ref[0] = dot(gated_ref[...], weight_ref[...]).astype(BF16)
+def project_kernel(spot_ref, gated_ref, weight_ref, *out_refs):
+    step = pl.program_id(0)
+    block = dot(gated_ref[...], weight_ref[...]).astype(BF16)
+    for turn, out_ref in enumerate(out_refs):
+
+        @pl.when(step // 2 == turn)
+        def _():
+            out_ref[0] = block
 
 
 def shape(dims, kind):
     return jax.ShapeDtypeStruct(dims, kind)
 
 
-def params(mebibytes=48):
+def params(mebibytes=16):
     return pltpu.CompilerParams(vmem_limit_bytes=mebibytes * 1024 * 1024)
 
 
@@ -214,7 +222,16 @@
         pack_kernel, out_shape=shape((shards, rows, INNER), BF16), compiler_params=params(), name="pack_pair"
     )(value_input, filter_taps)
     pair = exchange(pair, "seq")
-    grad_full = exchange(jnp.broadcast_to(grad_output[None], (groups, rows, channels)), "ch")
+    place = lax.axis_index("ch")
+    ring = groups // 2
+    spot = jnp.stack([place // 2, place % 2]).astype(jnp.int32)
+    halves = jnp.stack([grad_output[:, :width], grad_output[:, width:]])
+    across = lax.ppermute(halves, "ch", [(i, i ^ 1) for i in range(groups)])
+    even = spot[1] == 0
+    sides = jnp.concatenate([jnp.where(even, halves, across), jnp.where(even, across, halves)], 0)
+    grad_full = lax.all_gather(
+        sides, "ch", axis=0, tiled=True, axis_index_groups=[[2 * i + j for i in range(ring)] for j in range(2)]
+    )
 
     packed, spec = pl.pallas_call(
         convolve_kernel,
@@ -231,29 +248,25 @@
     )(exchange(packed, "seq"), gate_input)
     gated_all = lax.all_gather(gated, "seq", axis=0, tiled=True)
 
-    whole = lambda *dims: pl.BlockSpec(dims, lambda step: (0,) * len(dims))
-    pre_grad, cotangent, columns = pl.pallas_call(
+    whole = lambda *dims: pl.BlockSpec(dims, lambda step, spot: (0,) * len(dims))
+    columns = exchange(grad_full, "seq")
+    fixed = lambda *dims: pl.BlockSpec(dims, lambda step: (0,) * len(dims))
+    gate_grad, cotangent = pl.pallas_call(
         pre_grad_kernel,
         grid=(groups,),
         in_specs=[
-            pl.BlockSpec((1, rows, channels), lambda step: (step, 0, 0)),
+            pl.BlockSpec((shards // groups, rows, width), lambda step: (step, 0, 0)),
             pl.BlockSpec((channels, channels), lambda step: (0, step)),
-            whole(rows, channels),
+            fixed(rows, channels),
+            fixed(rows, channels),
         ],
-        out_specs=(
-            whole(rows, channels),
-            whole(shards, HALF, INNER),
-            pl.BlockSpec((shards // groups, rows, width), lambda step: (step, 0, 0)),
-        ),
-        out_shape=(
-            shape((rows, channels), F32),
-            shape((shards, HALF, INNER), BF16),
-            shape((shards, rows, width), BF16),
-        ),
-        compiler_params=params(),
+        out_specs=(fixed(rows, channels), fixed(shards, HALF, INNER)),
+        out_shape=(shape((rows, channels), BF16), shape((shards, HALF, INNER), BF16)),
+        scratch_shapes=[pltpu.VMEM((channels, rows), F32)],
+        compiler_params=params(52),
         name="pre_grad",
-    )(grad_full, out_weight, gate_input)
-    gate_grad = (pre_grad * conv).astype(BF16)
+    )(grad_full, out_weight, gate_input, conv)
+    cotangent, columns = lax.optimization_barrier((cotangent, columns))
 
     returned = pl.pallas_call(
         correlate_kernel,
@@ -269,18 +282,38 @@
         name="finish",
     )(exchange(returned, "seq"))
 
-    projected = pl.pallas_call(
+    order = (2, 1, 3, 0)
+
+    def weight_block(step, spot):
+        turn = step // 2
+        ahead = jnp.where(turn == 0, 2, jnp.where(turn == 1, 1, jnp.where(turn == 2, 3, 0)))
+        return 0, lax.rem(spot[0] + ahead, ring) * 2 + (step ^ spot[1]) % 2
+
+    def out_block(turn):
+        return lambda step, spot: (jnp.clip(step - 2 * turn, 0, 1), 0, 0)
+
+    parts = pl.pallas_call(
         project_kernel,
-        grid=(groups,),
-        in_specs=[whole(rows, channels), pl.BlockSpec((channels, channels), lambda step: (0, step))],
-        out_specs=pl.BlockSpec((1, rows, channels), lambda step: (step, 0, 0)),
-        out_shape=shape((groups, rows, channels), BF16),
-        compiler_params=params(),
+        grid_spec=pltpu.PrefetchScalarGridSpec(
+            num_scalar_prefetch=1,
+            grid=(groups,),
+            in_specs=[whole(rows, channels), pl.BlockSpec((channels, channels), weight_block)],
+            out_specs=[pl.BlockSpec((1, rows, channels), out_block(turn)) for turn in range(ring)],
+        ),
+        out_shape=[shape((2, rows, channels), BF16)] * ring,
+        compiler_params=params(52),
         name="project",
-    )(gated, out_weight)
-    block_output = jnp.sum(exchange(projected, "ch").astype(F32), axis=0).astype(BF16)
-
-    columns = exchange(columns, "seq").reshape(shards * rows, width)
+    )(spot, gated, out_weight)
+    parts = [
+        lax.ppermute(part, "ch", [(i, (i + 2 * ahead) % groups) for i in range(groups)]) if ahead else part
+        for part, ahead in zip(parts, order)
+    ]
+    far = sum(part[1].astype(F32) for part in parts).astype(BF16)
+    near = sum(part[0].astype(F32) for part in parts)
+    far = lax.ppermute(far, "ch", [(i, i ^ 1) for i in range(groups)])
+    block_output = (near + far.astype(F32)).astype(BF16)
+
+    columns = columns.reshape(shards * rows, width)
     summed = lax.dot_general(gated_all, columns, (((0,), (0,)), ((), ())), preferred_element_type=F32)
     weight_grad = (summed * scale).astype(BF16)
     return (block_output, gate_grad, value_grad, filter_grad, weight_grad)

time: 225 us -> 147 us (0.65)
  blocking collectives: 124 us -> 27.3 us
  starting transfers between devices: 11.7 us -> 28.1 us
    all_to_all x5 -> x2, blocking collectives: 124 us -> 27.3 us  [exchange(): return lax.all_to_all(array, axis, split_axis=0, concat_axis=0, tiled=True)]
    ppermute x0 -> x5, starting transfers between devices: none -> 11.5 us  [the longest x3 5.03 us: body(): lax.ppermute(part, 'ch', [(i, (i + 2 * ahead) % groups) for i in range(gr...]
    all_to_all x2 -> x3, waiting for transfers between devices: 23.1 us -> 15.8 us  [exchange(): return lax.all_to_all(array, axis, split_axis=0, concat_axis=0, tiled=True)]
    ppermute x0 -> x5, waiting for transfers between devices: none -> 5.76 us  [the longest x1 5.75 us: body(): across = lax.ppermute(halves, 'ch', [(i, i ^ 1) for i in range(groups)])]
    all_to_all x2 -> x3, starting transfers between devices: 11.7 us -> 16.5 us  [exchange(): return lax.all_to_all(array, axis, split_axis=0, concat_axis=0, tiled=True)]
    pallas_call x2, Pallas kernels: 20.7 us -> 23.5 us  [the longest x1 12.1 us: body(): pl.pallas_call(pre_grad_kernel, grid=(groups,), in_specs=[pl.BlockSpec((s...]
    reduce_sum x1 -> x0, other arithmetic: 2.72 us -> none  [body(): jnp.sum(exchange(projected, 'ch').astype(F32), axis=0).astype(BF16)]
  transfers between devices with their start and end apart: 3 -> 10, of which waited for: 1 -> 4; matrix products, arithmetic and copies ran while one was open for 2% -> 3% of each run, Pallas kernels for 12% -> 22%
where the time goes in v1:
time: 147 us; the launch traced here: 146 us
  Pallas kernels  32.2 us (22%)
  starting transfers between devices  28.1 us (19%)
  blocking collectives  27.3 us (19%)
  waiting for transfers between devices  21.6 us (15%)
  between operations  14.2 us (10%)
  local copies, waits for them, and re-layouts  11.2 us (8%)
  matrix products  6.2 us (4%)
  other arithmetic  5.23 us (4%)
    all_to_all x2, blocking collectives, exchange(): return lax.all_to_all(array, axis, split_axis=0, concat_axis=0, tiled=True)  27.3 us
    all_to_all x3, starting transfers between devices, exchange(): return lax.all_to_all(array, axis, split_axis=0, concat_axis=0, tiled=True)  16.5 us
    all_to_all x3, waiting for transfers between devices, exchange(): return lax.all_to_all(array, axis, split_axis=0, concat_axis=0, tiled=True)  15.8 us
    pallas_call x1, Pallas kernels, body(): pl.pallas_call(pre_grad_kernel, grid=(groups,), in_specs=[pl.BlockSpec((s...  12.1 us
    pallas_call x1, Pallas kernels, body(): pl.pallas_call(project_kernel, grid_spec=pltpu.PrefetchScalarGridSpec(num...  11.4 us
    unnamed x32, local copies, waits for them, and re-layouts  10.2 us
    dot_general x1, matrix products, body(): lax.dot_general(gated_all, columns, (((0,), (0,)), ((), ())), preferred_e...  6.2 us
    ppermute x1, waiting for transfers between devices, body(): across = lax.ppermute(halves, 'ch', [(i, i ^ 1) for i in range(groups)])  5.75 us
  transfers between devices with their start and end apart: 10, of which 4 were waited for; matrix products, arithmetic and copies ran while one was open for 3% of the time, Pallas kernels for 22%

profile of v1, /device:TPU:1, one launch (start us, length us, event | category | flops | bytes accessed | tf_op | source)
XLA Modules:
  0.0 146.0 jit_solution(10972585330880576645)
XLA Ops:
  7.2 0.0 copy-start.14
  7.2 0.0 copy-start.13
  7.2 0.0 all-gather.3.cloned.1.call-start
  7.2 1.0 slice_bitcast_fusion.1
  8.3 3.8 %collective-permute-start.4 = (bf16[2,128,512]{2,1,0:T(8,128)(2,1)S(1)}, bf16[2,128,512]{2,1,0:T(8,128)(2,1)S(1)}, u32[]{:S(2)}, u32[]{:S(2)}) collective-permute-start(bf16[2,128,512]{2,1,0:T(8,128)(2,1)S(1)} %pad_maximum_fusion.1), channel_id=1, source_target_pairs={{0,1},{1,0},{2,3},{3,2},{4,5},{5,4},{6,7},{7,6},{8,9},{9,8},{10,11... | collective-permute-start | bytes 786440 | tf_op jit(solution)/shard_map/ppermute | solution.py:229
  12.1 5.8 %collective-permute-done.4 = bf16[2,128,512]{2,1,0:T(8,128)(2,1)S(1)} collective-permute-done((bf16[2,128,512]{2,1,0:T(8,128)(2,1)S(1)}, bf16[2,128,512]{2,1,0:T(8,128)(2,1)S(1)}, u32[]{:S(2)}, u32[]{:S(2)}) %collective-permute-start.4) | collective-permute-done | bytes 262176 | tf_op jit(solution)/shard_map/ppermute | solution.py:229
  17.9 0.0 copy-start
  17.9 0.8 pad_maximum_fusion
  18.8 0.0 all-gather.3.cloned.1.call-update
  18.8 0.0 all-gather.5.cloned.1.call-start
  18.9 0.0 copy-done.14
  18.9 0.0 copy-done.13
  18.9 0.2 pack_pair.1
  19.1 16.6 %all_to_all.25.pair_ref = bf16[16,128,128]{2,1,0:T(8,128)(2,1)S(1)} all-to-all(bf16[16,128,128]{2,1,0:T(8,128)(2,1)S(1)} %pack_pair.1), channel_id=1, replica_groups=mesh['seq'=16,'ch'=8] {'seq'}, dimensions={0} | all-to-all | bytes 1048576 | tf_op jit(solution)/shard_map/all_to_all | solution.py:208
  35.7 0.0 copy-done
  35.7 0.0 copy-start.1
  35.7 1.6 %copy-done.1 = bf16[17,256,256]{2,1,0:T(8,128)(2,1)S(1)} copy-done((bf16[17,256,256]{2,1,0:T(8,128)(2,1)S(1)}, bf16[17,256,256]{2,1,0:T(8,128)(2,1)}, u32[]{:S(2)}) %copy-start.1) | copy-done | bytes 2228248
  37.3 0.0 copy-start.7
  37.3 0.9 copy-done.7
  38.2 0.0 copy-start.9
  38.3 1.0 copy-done.9
  39.2 0.0 copy-start.3
  39.2 2.7 %convolve.1 = (bf16[16,64,128]{2,1,0:T(8,128)(2,1)S(1)}, bf16[17,256,128]{2,1,0:T(8,128)(2,1)S(1)}) custom-call(bf16[16,128,128]{2,1,0:T(8,128)(2,1)S(1)} %all_to_all.25.pair_ref, bf16[512,256]{1,0:T(8,128)(2,1)S(1)} %copy-done.7, bf16[17,256,256]{2,1,0:T(8,128)(2,1)S(1)} %copy-done, bf16[17,256,256]{2,1,0:T(8,128)(2,1)S(1)} %copy-done.1, ...), custom_call_target="tpu_custom_call" | custom-call | tf_op jit(solution)/shard_map/convolve/pallas_call | solution.py:236
  41.9 10.7 %all_to_all.26.recv_ref = bf16[16,64,128]{2,1,0:T(8,128)(2,1)S(1)} all-to-all(bf16[16,64,128]{2,1,0:T(8,128)(2,1)S(1)} %get-tuple-element.19), channel_id=1, replica_groups=mesh['seq'=16,'ch'=8] {'seq'}, dimensions={0} | all-to-all | bytes 524288 | tf_op jit(solution)/shard_map/all_to_all | solution.py:208
  52.7 0.0 copy-done.3
  52.7 0.2 gate.1
  52.9 0.0 copy-start.5
  52.9 0.7 copy-done.5
  53.5 0.0 copy-start.11
  53.5 0.8 copy-done.11
  54.3 0.0 all-gather.5.cloned.1.call-update
  54.4 0.0 all-gather.3.cloned.1.call-done.grad_ref
  54.4 5.0 %all-to-all-start.2 = ((bf16[16,128,512]{2,1,0:T(8,128)(2,1)}), bf16[16,128,512]{2,1,0:T(8,128)(2,1)}, u32[]{:S(2)}, u32[]{:S(2)}) async-start(bf16[16,128,512]{2,1,0:T(8,128)(2,1)} %all-gather.3.cloned.1.call-done.grad_ref), calls=%async_computation.2 | async-start | bytes 4194304 | tf_op jit(solution)/shard_map/all_to_all | solution.py:208
  59.4 0.1 pad_add_fusion.spot_ref
  59.5 0.0 copy-start.6
  59.5 0.9 copy-done.6
  60.4 0.0 copy-start.4
  60.4 0.0 copy-start.12
  60.4 11.4 %project.1 = (bf16[2,128,1024]{2,1,0:T(8,128)(2,1)}, bf16[2,128,1024]{2,1,0:T(8,128)(2,1)}, bf16[2,128,1024]{2,1,0:T(8,128)(2,1)}, bf16[2,128,1024]{2,1,0:T(8,128)(2,1)}) custom-call(s32[2]{0:T(128)S(1)} %pad_add_fusion.spot_ref, bf16[128,1024]{1,0:T(8,128)(2,1)S(1)} %copy-done.6, bf16[1024,8192]{1,0:T(8,128)(2,1)} %weight_ref.3), custom_call_target="tpu_custom_call" | custom-call | tf_op jit(solution)/shard_map/project/pallas_call | solution.py:295
  71.8 3.7 %collective-permute-start.2 = (bf16[2,128,1024]{2,1,0:T(8,128)(2,1)}, bf16[2,128,1024]{2,1,0:T(8,128)(2,1)}, u32[]{:S(2)}, u32[]{:S(2)}) collective-permute-start(bf16[2,128,1024]{2,1,0:T(8,128)(2,1)} %get-tuple-element.23), channel_id=1, source_target_pairs={{0,6},{1,7},{2,0},{3,1},{4,2},{5,3},{6,4},{7,5},{8,14},{9,15},{10,... | collective-permute-start | bytes 1572872 | tf_op jit(solution)/shard_map/ppermute | solution.py:308
  75.5 0.0 collective-permute-start.1
  75.5 1.4 collective-permute-start
  76.9 0.0 copy-done.4
  76.9 0.0 copy-done.12
  76.9 12.1 %pre_grad.1 = (bf16[128,1024]{1,0:T(8,128)(2,1)}, bf16[16,64,128]{2,1,0:T(8,128)(2,1)S(1)}) custom-call(bf16[16,128,512]{2,1,0:T(8,128)(2,1)} %all-gather.3.cloned.1.call-done.grad_ref, bf16[1024,8192]{1,0:T(8,128)(2,1)} %weight_ref.3, bf16[128,1024]{1,0:T(8,128)(2,1)S(1)} %copy-done.4, f32[128,1024]{1,0:T(8,128)S(1)} %copy-done.12), custom_call_target="tpu_custom_call" | custom-call | tf_op jit(solution)/shard_map/pre_grad/pallas_call | solution.py:254
  88.9 0.7 copy-done.15
  89.6 4.1 %all-to-all-done.2 = bf16[16,128,512]{2,1,0:T(8,128)(2,1)} async-done(((bf16[16,128,512]{2,1,0:T(8,128)(2,1)}), bf16[16,128,512]{2,1,0:T(8,128)(2,1)}, u32[]{:S(2)}, u32[]{:S(2)}) %all-to-all-start.2) | async-done | bytes 2097184 | tf_op jit(solution)/shard_map/all_to_all | solution.py:208
  93.8 7.6 %all-to-all-start.3 = ((bf16[16,64,128]{2,1,0:T(8,128)(2,1)}), bf16[16,64,128]{2,1,0:T(8,128)(2,1)}, u32[]{:S(2)}, u32[]{:S(2)}) async-start(bf16[16,64,128]{2,1,0:T(8,128)(2,1)} %copy-done.15), calls=%async_computation.3 | async-start | bytes 524288 | tf_op jit(solution)/shard_map/all_to_all | solution.py:208
  101.4 0.0 collective-permute-done.2
  101.4 0.0 collective-permute-done.1
  101.4 0.0 collective-permute-done
  101.4 2.1 %fusion.1 = bf16[128,1024]{1,0:T(8,128)(2,1)} fusion(bf16[2,128,1024]{2,1,0:T(8,128)(2,1)} %collective-permute-done.2, bf16[2,128,1024]{2,1,0:T(8,128)(2,1)} %collective-permute-done.1, bf16[2,128,1024]{2,1,0:T(8,128)(2,1)} %collective-permute-done, bf16[2,128,1024]{2,1,0:T(8,128)(2,1)} %get-tuple-element.24), kind=kLoop, calls=%fused_computation.5 | loop fusion | flops 1048576 | bytes 1310720 | tf_op jit(solution)/shard_map/add | solution.py:311
  103.4 2.6 %collective-permute-start.3 = (bf16[128,1024]{1,0:T(8,128)(2,1)}, bf16[128,1024]{1,0:T(8,128)(2,1)}, u32[]{:S(2)}, u32[]{:S(2)}) collective-permute-start(bf16[128,1024]{1,0:T(8,128)(2,1)} %fusion.1), channel_id=1, source_target_pairs={{0,1},{1,0},{2,3},{3,2},{4,5},{5,4},{6,7},{7,6},{8,9},{9,8},{10,11... | collective-permute-start | bytes 786440 | tf_op jit(solution)/shard_map/ppermute | solution.py:313
  106.0 3.9 %all-to-all-done.3.grad_ref = bf16[16,64,128]{2,1,0:T(8,128)(2,1)} async-done(((bf16[16,64,128]{2,1,0:T(8,128)(2,1)}), bf16[16,64,128]{2,1,0:T(8,128)(2,1)}, u32[]{:S(2)}, u32[]{:S(2)}) %all-to-all-start.3) | async-done | bytes 262176 | tf_op jit(solution)/shard_map/all_to_all | solution.py:208
  110.0 1.6 %copy-done.2 = bf16[17,256,256]{2,1,0:T(8,128)(2,1)S(1)} copy-done((bf16[17,256,256]{2,1,0:T(8,128)(2,1)S(1)}, bf16[17,256,256]{2,1,0:T(8,128)(2,1)}, u32[]{:S(2)}) %copy-start.2) | copy-done | bytes 2228248
  111.6 0.9 copy-done.8
  112.6 0.9 copy-done.10
  113.5 4.5 %correlate.1 = bf16[16,128,128]{2,1,0:T(8,128)(2,1)} custom-call(bf16[16,64,128]{2,1,0:T(8,128)(2,1)} %all-to-all-done.3.grad_ref, bf16[17,256,128]{2,1,0:T(8,128)(2,1)S(1)} %get-tuple-element.29.spec_ref, bf16[512,256]{1,0:T(8,128)(2,1)S(1)} %copy-done.8, bf16[17,256,256]{2,1,0:T(8,128)(2,1)S(1)} %copy-done, bf16[17,256,256]{2,1,0:T(8,128)(2,1)S(1)} %copy-done.2, ...), custom_call_target="tpu_custom_call" | custom-call | tf_op jit(solution)/shard_map/correlate/pallas_call | solution.py:271
  118.0 4.0 %all-to-all-start.4 = ((bf16[16,128,128]{2,1,0:T(8,128)(2,1)}), bf16[16,128,128]{2,1,0:T(8,128)(2,1)S(1)}, u32[]{:S(2)}, u32[]{:S(2)}) async-start(bf16[16,128,128]{2,1,0:T(8,128)(2,1)} %correlate.1), calls=%async_computation.4 | async-start | bytes 1048576 | tf_op jit(solution)/shard_map/all_to_all | solution.py:208
  122.0 0.0 collective-permute-done.3
  122.0 2.2 %fusion = bf16[128,1024]{1,0:T(8,128)(2,1)} fusion(bf16[128,1024]{1,0:T(8,128)(2,1)} %collective-permute-done.3, bf16[2,128,1024]{2,1,0:T(8,128)(2,1)} %collective-permute-done.2, bf16[2,128,1024]{2,1,0:T(8,128)(2,1)} %collective-permute-done.1, bf16[2,128,1024]{2,1,0:T(8,128)(2,1)} %collective-permute-done, bf16[2,128,1024]{2,1,0:T(8,128)(2,1)} %get-tuple-element.24), kind=kLoop, calls=%fused_computation.3 | loop fusion | flops 1310720 | bytes 1572864 | tf_op jit(solution)/shard_map/convert_element_type | solution.py:314
  124.2 7.7 %all-to-all-done.4.recv_ref = bf16[16,128,128]{2,1,0:T(8,128)(2,1)S(1)} async-done(((bf16[16,128,128]{2,1,0:T(8,128)(2,1)}), bf16[16,128,128]{2,1,0:T(8,128)(2,1)S(1)}, u32[]{:S(2)}, u32[]{:S(2)}) %all-to-all-start.4) | async-done | bytes 524320 | tf_op jit(solution)/shard_map/all_to_all | solution.py:208
  131.9 1.1 finish.1
  133.0 6.2 %multiply_convert_fusion = bf16[1024,512]{1,0:T(8,128)(2,1)} fusion(bf16[2048,1024]{1,0:T(8,128)(2,1)} %all-gather.5.cloned.1.call-done, bf16[2048,512]{1,0:T(8,128)(2,1)} %bitcast.6), kind=kOutput, calls=%fused_computation | convolution fusion | flops 2148532224 | bytes 7340032 | tf_op jit(solution)/shard_map/dot_general | solution.py:317
  (7 shorter events, 0.1 us)
Async XLA Ops:
  7.2 11.7 %copy-start.14 = (bf16[128,1024]{1,0:T(8,128)(2,1)S(1)}, bf16[128,1024]{1,0:T(8,128)(2,1)}, u32[]{:S(2)}) copy-start(bf16[128,1024]{1,0:T(8,128)(2,1)} %value_ref.1) | copy-start | bytes 786436
  7.2 11.7 %copy-start.13 = (f32[128,1024]{1,0:T(8,128)S(1)}, f32[128,1024]{1,0:T(8,128)}, u32[]{:S(2)}) copy-start(f32[128,1024]{1,0:T(8,128)} %taps_ref.1) | copy-start | bytes 1572868
  7.2 47.2 %all-gather.3.cloned.1.call-start = ((), (), s32[]{:S(2)}) async-start(), calls=%async_computation.5 | async-start | bytes 2621440 | tf_op jit(solution)/shard_map/all_gather | solution.py:232
  8.3 9.6 %collective-permute-start.4 = (bf16[2,128,512]{2,1,0:T(8,128)(2,1)S(1)}, bf16[2,128,512]{2,1,0:T(8,128)(2,1)S(1)}, u32[]{:S(2)}, u32[]{:S(2)}) collective-permute-start(bf16[2,128,512]{2,1,0:T(8,128)(2,1)S(1)} %pad_maximum_fusion.1), channel_id=1, source_target_pairs={{0,1},{1,0},{2,3},{3,2},{4,5},{5,4},{6,7},{7,6},{8,9},{9,8},{10,11... | collective-permute-start | bytes 786440 | tf_op jit(solution)/shard_map/ppermute | solution.py:229
  17.9 17.7 %copy-start = (bf16[17,256,256]{2,1,0:T(8,128)(2,1)S(1)}, bf16[17,256,256]{2,1,0:T(8,128)(2,1)}, u32[]{:S(2)}) copy-start(bf16[17,256,256]{2,1,0:T(8,128)(2,1)} %constant.41.clone.inner_ref) | copy-start | bytes 6684676
  18.8 114.2 %all-gather.5.cloned.1.call-start = ((), (), s32[]{:S(2)}) async-start(), calls=%async_computation.6 | async-start | bytes 4456448 | tf_op jit(solution)/shard_map/all_gather | solution.py:249
  35.7 1.6 %copy-start.1 = (bf16[17,256,256]{2,1,0:T(8,128)(2,1)S(1)}, bf16[17,256,256]{2,1,0:T(8,128)(2,1)}, u32[]{:S(2)}) copy-start(bf16[17,256,256]{2,1,0:T(8,128)(2,1)} %constant.42.clone.inner_back_ref) | copy-start | bytes 6684676
  37.3 0.9 copy-start.7
  38.2 1.0 copy-start.9
  39.2 13.5 %copy-start.3 = (bf16[128,1024]{1,0:T(8,128)(2,1)S(1)}, bf16[128,1024]{1,0:T(8,128)(2,1)}, u32[]{:S(2)}) copy-start(bf16[128,1024]{1,0:T(8,128)(2,1)} %gate_ref.3) | copy-start | bytes 786436
  52.9 0.7 copy-start.5
  53.5 0.8 copy-start.11
  54.4 39.4 %all-to-all-start.2 = ((bf16[16,128,512]{2,1,0:T(8,128)(2,1)}), bf16[16,128,512]{2,1,0:T(8,128)(2,1)}, u32[]{:S(2)}, u32[]{:S(2)}) async-start(bf16[16,128,512]{2,1,0:T(8,128)(2,1)} %all-gather.3.cloned.1.call-done.grad_ref), calls=%async_computation.2 | async-start | bytes 4194304 | tf_op jit(solution)/shard_map/all_to_all | solution.py:208
  59.5 0.9 copy-start.6
  60.4 16.5 %copy-start.4 = (bf16[128,1024]{1,0:T(8,128)(2,1)S(1)}, bf16[128,1024]{1,0:T(8,128)(2,1)}, u32[]{:S(2)}) copy-start(bf16[128,1024]{1,0:T(8,128)(2,1)} %gate_ref.3) | copy-start | bytes 786436
  60.4 16.5 %copy-start.12 = (f32[128,1024]{1,0:T(8,128)S(1)}, f32[128,1024]{1,0:T(8,128)}, u32[]{:S(2)}) copy-start(f32[128,1024]{1,0:T(8,128)} %copy-done.11) | copy-start | bytes 1572868
  71.8 29.5 %collective-permute-start.2 = (bf16[2,128,1024]{2,1,0:T(8,128)(2,1)}, bf16[2,128,1024]{2,1,0:T(8,128)(2,1)}, u32[]{:S(2)}, u32[]{:S(2)}) collective-permute-start(bf16[2,128,1024]{2,1,0:T(8,128)(2,1)} %get-tuple-element.23), channel_id=1, source_target_pairs={{0,6},{1,7},{2,0},{3,1},{4,2},{5,3},{6,4},{7,5},{8,14},{9,15},{10,... | collective-permute-start | bytes 1572872 | tf_op jit(solution)/shard_map/ppermute | solution.py:308
  75.5 25.9 %collective-permute-start.1 = (bf16[2,128,1024]{2,1,0:T(8,128)(2,1)}, bf16[2,128,1024]{2,1,0:T(8,128)(2,1)}, u32[]{:S(2)}, u32[]{:S(2)}) collective-permute-start(bf16[2,128,1024]{2,1,0:T(8,128)(2,1)} %get-tuple-element.22), channel_id=1, source_target_pairs={{0,2},{1,3},{2,4},{3,5},{4,6},{5,7},{6,0},{7,1},{8,10},{9,11},{10,... | collective-permute-start | bytes 1572872 | tf_op jit(solution)/shard_map/ppermute | solution.py:308
  75.5 25.9 %collective-permute-start = (bf16[2,128,1024]{2,1,0:T(8,128)(2,1)}, bf16[2,128,1024]{2,1,0:T(8,128)(2,1)}, u32[]{:S(2)}, u32[]{:S(2)}) collective-permute-start(bf16[2,128,1024]{2,1,0:T(8,128)(2,1)} %get-tuple-element.21), channel_id=1, source_target_pairs={{0,4},{1,5},{2,6},{3,7},{4,0},{5,1},{6,2},{7,3},{8,12},{9,13},{10,... | collective-permute-start | bytes 1572872 | tf_op jit(solution)/shard_map/ppermute | solution.py:308
  88.9 0.7 copy-start.15
  93.8 16.2 %all-to-all-start.3 = ((bf16[16,64,128]{2,1,0:T(8,128)(2,1)}), bf16[16,64,128]{2,1,0:T(8,128)(2,1)}, u32[]{:S(2)}, u32[]{:S(2)}) async-start(bf16[16,64,128]{2,1,0:T(8,128)(2,1)} %copy-done.15), calls=%async_computation.3 | async-start | bytes 524288 | tf_op jit(solution)/shard_map/all_to_all | solution.py:208
  103.4 18.5 %collective-permute-start.3 = (bf16[128,1024]{1,0:T(8,128)(2,1)}, bf16[128,1024]{1,0:T(8,128)(2,1)}, u32[]{:S(2)}, u32[]{:S(2)}) collective-permute-start(bf16[128,1024]{1,0:T(8,128)(2,1)} %fusion.1), channel_id=1, source_target_pairs={{0,1},{1,0},{2,3},{3,2},{4,5},{5,4},{6,7},{7,6},{8,9},{9,8},{10,11... | collective-permute-start | bytes 786440 | tf_op jit(solution)/shard_map/ppermute | solution.py:313
  110.0 1.6 %copy-start.2 = (bf16[17,256,256]{2,1,0:T(8,128)(2,1)S(1)}, bf16[17,256,256]{2,1,0:T(8,128)(2,1)}, u32[]{:S(2)}) copy-start(bf16[17,256,256]{2,1,0:T(8,128)(2,1)} %constant.42.clone.inner_back_ref) | copy-start | bytes 6684676
  111.6 0.9 copy-start.8
  112.6 0.9 copy-start.10
  118.0 13.8 %all-to-all-start.4 = ((bf16[16,128,128]{2,1,0:T(8,128)(2,1)}), bf16[16,128,128]{2,1,0:T(8,128)(2,1)S(1)}, u32[]{:S(2)}, u32[]{:S(2)}) async-start(bf16[16,128,128]{2,1,0:T(8,128)(2,1)} %correlate.1), calls=%async_computation.4 | async-start | bytes 1048576 | tf_op jit(solution)/shard_map/all_to_all | solution.py:208
Sparse Core Ops, SparseCore 0:
  18.9 34.3 all-gather.2
  55.0 57.1 all-gather.4

commit v2 on v0

v2 whole, which is shorter than its diff:
```python
import functools
import math

import jax
import jax.numpy as jnp
import numpy as np
from jax import lax
from jax.experimental import pallas as pl
from jax.experimental.pallas import tpu as pltpu
from jax.sharding import PartitionSpec as P

BLOCKS = 16
INNER = 128
PERIOD = 2 * BLOCKS * INNER
HALF = 64
GROUP = 16
BF16 = jnp.bfloat16
F32 = jnp.float32


def plane_order():
    order = [(0, False), (BLOCKS, False)]
    for freq in range(1, BLOCKS):
        order += [(freq, False), (freq, True)]
    return order


def outer_matrices():
    blocks = np.arange(BLOCKS)
    forward = np.zeros((2 * BLOCKS, BLOCKS))
    inverse = np.zeros((BLOCKS, 2 * BLOCKS))
    for plane, (freq, imaginary) in enumerate(plane_order()):
        turn = 2.0 * np.pi * ((freq * blocks) % (2 * BLOCKS)) / (2 * BLOCKS)
        weight = (1.0 if freq in (0, BLOCKS) else 2.0) / PERIOD
        wave = -np.sin(turn) if imaginary else np.cos(turn)
        forward[plane] = wave
        inverse[:, plane] = weight * wave
    eye = np.eye(GROUP)
    return np.kron(forward, eye), np.kron(inverse, eye)


def inner_matrices():
    freqs = np.arange(BLOCKS + 1)[:, None, None] + 2 * BLOCKS * np.arange(INNER)[None, :, None]
    turn = 2.0 * np.pi * ((freqs * np.arange(INNER)[None, None, :]) % PERIOD) / PERIOD
    cos, sin = np.cos(turn), np.sin(turn)
    back = [np.swapaxes(wave, 1, 2) for wave in (cos, sin)]
    return np.concatenate([cos, sin], axis=1), np.concatenate(back, axis=1)


def dot(left, right):
    return jnp.dot(left, right, preferred_element_type=F32)


def lane_low(shape):
    return lax.broadcasted_iota(jnp.int32, shape, len(shape) - 1) < HALF


def swap(array):
    return pltpu.roll(array, HALF, array.ndim - 1)


def pack_kernel(value_ref, taps_ref, out_ref):
    for pair in range(value_ref.shape[1] // INNER):
        lanes = pl.ds(pair * INNER, INNER)
        value = value_ref[:, lanes].astype(F32)
        taps = taps_ref[:, lanes]
        low = lane_low(value.shape)
        out_ref[2 * pair] = jnp.where(low, value, swap(taps)).astype(BF16)
        out_ref[2 * pair + 1] = jnp.where(low, swap(value), taps).astype(BF16)


def fold_rows(block):
    top, bottom = block[:HALF], block[HALF:]
    low = lane_low(top.shape)
    return jnp.where(low, top, swap(bottom)), jnp.where(low, swap(top), bottom)


def unfold_rows(first, second):
    low = lane_low(first.shape)
    return jnp.concatenate([jnp.where(low, first, swap(second)), jnp.where(low, swap(first), second)], 0)


def side_by_side(table_ref, first, count):
    return jnp.concatenate([table_ref[first + i] for i in range(count)], 1)


def outer_forward(read_group, table_ref, planes_ref):
    start = 2 * (BLOCKS + 1)
    for group in range(INNER // GROUP):
        rows = pl.ds(group * GROUP, GROUP)
        block = read_group(rows).reshape(BLOCKS * GROUP, INNER)
        for half in range(2):
            wide = dot(side_by_side(table_ref, start + 2 * half, 2), block).astype(BF16)
            planes_ref[pl.ds(half * BLOCKS, BLOCKS), rows, :] = wide.reshape(BLOCKS, GROUP, INNER)


def inner_forward(freq, table_ref, planes_ref):
    if freq in (0, BLOCKS):
        both = dot(table_ref[freq], planes_ref[0 if freq == 0 else 1])
        return both[:INNER], -both[INNER:]
    both = dot(table_ref[freq], jnp.concatenate([planes_ref[2 * freq], planes_ref[2 * freq + 1]], 1))
    return both[:INNER, :INNER] + both[INNER:, INNER:], both[:INNER, INNER:] - both[INNER:, :INNER]


def inner_inverse(freq, re, im, table_ref, planes_ref):
    both = dot(table_ref[BLOCKS + 1 + freq], jnp.concatenate([re.astype(BF16), im.astype(BF16)], 1))
    back_re = (both[:INNER, :INNER] - both[INNER:, INNER:]).astype(BF16)
    if freq in (0, BLOCKS):
        planes_ref[0 if freq == 0 else 1] = back_re
    else:
        planes_ref[2 * freq] = back_re
        planes_ref[2 * freq + 1] = (both[INNER:, :INNER] + both[:INNER, INNER:]).astype(BF16)


def outer_inverse(group, table_ref, planes_ref):
    planes = planes_ref[:, pl.ds(group * GROUP, GROUP), :].reshape(2 * BLOCKS * GROUP, INNER)
    return dot(side_by_side(table_ref, 2 * (BLOCKS + 1) + 4, 4), planes).reshape(BLOCKS, GROUP, INNER)


def transform_table():
    outer, outer_back = outer_matrices()
    blocks = list(inner_matrices())
    for half in range(2):
        rows = outer[half * 2 * INNER : (half + 1) * 2 * INNER]
        blocks.append(np.stack([rows[:, :INNER], rows[:, INNER:]]))
    blocks.append(np.stack(np.split(outer_back, 4, axis=1)))
    return np.concatenate(blocks)


def convolve_kernel(pair_ref, table_ref, out_ref, spec_hbm, spec_ref, planes_ref, back_ref, semaphore):
    outer_forward(lambda rows: pair_ref[:, rows, :], table_ref, planes_ref)
    for freq in range(BLOCKS + 1):
        re, im = inner_forward(freq, table_ref, planes_ref)
        spec_ref[freq, :INNER] = re.astype(BF16)
        spec_ref[freq, INNER:] = im.astype(BF16)
        other_re, other_im = swap(re), swap(im)
        inner_inverse(freq, re * other_re - im * other_im, re * other_im + im * other_re, table_ref, back_ref)
    send = pltpu.make_async_copy(spec_ref, spec_hbm, semaphore)
    send.start()
    half_groups = INNER // GROUP // 2
    for group in range(half_groups):
        one = outer_inverse(group, table_ref, back_ref)
        two = outer_inverse(group + half_groups, table_ref, back_ref)
        packed = jnp.where(lane_low(one.shape), one, two)
        out_ref[:, pl.ds(group * GROUP, GROUP), :] = packed.astype(BF16)
    send.wait()


def correlate_kernel(grad_ref, spec_hbm, table_ref, out_ref, spec_ref, wide_ref, planes_ref, back_ref, semaphore):
    load = pltpu.make_async_copy(spec_hbm, spec_ref, semaphore)
    load.start()
    for block in range(BLOCKS):
        packed = grad_ref[block].astype(F32)
        turned = swap(packed)
        low = lane_low(packed.shape)
        wide_ref[block, :HALF] = jnp.where(low, packed, turned).astype(BF16)
        wide_ref[block, HALF:] = jnp.where(low, turned, packed).astype(BF16)
    outer_forward(lambda rows: wide_ref[:, rows, :], table_ref, planes_ref)
    load.wait()
    for freq in range(BLOCKS + 1):
        grad_re, grad_im = inner_forward(freq, table_ref, planes_ref)
        re, im = spec_ref[freq, :INNER].astype(F32), spec_ref[freq, INNER:].astype(F32)
        inner_inverse(freq, re * grad_re + im * grad_im, re * grad_im - im * grad_re, table_ref, back_ref)
    for group in range(INNER // GROUP):
        out_ref[:, pl.ds(group * GROUP, GROUP), :] = outer_inverse(group, table_ref, back_ref).astype(BF16)


def fetch(pairs, semaphores):
    copies = [pltpu.make_async_copy(source, target, semaphores.at[i]) for i, (source, target) in enumerate(pairs)]
    for copy in copies:
        copy.start()
    return copies


def gate_kernel(recv_ref, gate_ref, conv_ref, gated_ref):
    for pair in range(BLOCKS // 2):
        conv = unfold_rows(recv_ref[2 * pair].astype(F32), recv_ref[2 * pair + 1].astype(F32))
        lanes = pl.ds(pair * INNER, INNER)
        conv_ref[:, lanes] = conv
        gated_ref[:, lanes] = (gate_ref[:, lanes].astype(F32) * conv).astype(BF16)


def finish_kernel(scale, recv_ref, value_grad_ref, filter_grad_ref):
    for pair in range(BLOCKS // 2):
        first = recv_ref[2 * pair].astype(F32)
        second = recv_ref[2 * pair + 1].astype(F32)
        low = lane_low(first.shape)
        lanes = pl.ds(pair * INNER, INNER)
        filter_grad_ref[:, lanes] = jnp.where(low, first, swap(second)) * scale
        value_grad_ref[:, lanes] = jnp.where(low, swap(first), second).astype(BF16)


def stream_weight(weight_hbm, block_column, buffers, semaphores, count, use):
    depth, _, width = buffers.shape

    def copy(step):
        columns = pl.ds(pl.multiple_of(block_column(step) * width, width), width)
        return pltpu.make_async_copy(weight_hbm.at[:, columns], buffers.at[step % depth], semaphores.at[step % depth])

    for step in range(depth - 1):
        copy(step).start()
    for step in range(count):
        if step + depth - 1 < count:
            copy(step + depth - 1).start()
        copy(step).wait()
        use(step, buffers.at[step % depth])


def grad_column(spot_ref, block):
    return block // 2 * 2 + lax.rem(spot_ref[1] + block % 2, 2)


def columns_kernel(spot_ref, grad_ref, out_ref):
    blocks, rows, channels = grad_ref.shape
    split = channels // 4
    quarter = rows // 4
    part = pl.ds(pl.multiple_of(spot_ref[0] * quarter, quarter), quarter)
    for block in range(blocks):
        for half in range(2):
            target = 2 * grad_column(spot_ref, block) + half
            start = 2 * half * split
            out_ref[target, :rows] = grad_ref[block, :, start : start + split]
            out_ref[target, rows:] = grad_ref[block, part, start + split : start + 2 * split]


def pre_grad_kernel(spot_ref, grad_ref, weight_hbm, gate_ref, total_ref, cotangent_ref, buffers, semaphores):
    def use(step, weight):
        part = lax.dot_general(grad_ref[step], weight[...], (((1,), (1,)), ((), ())), preferred_element_type=F32)
        total_ref[...] = part if step == 0 else total_ref[...] + part

    column = functools.partial(grad_column, spot_ref)
    stream_weight(weight_hbm, column, buffers, semaphores, grad_ref.shape[0], use)
    for pair in range(BLOCKS // 2):
        lanes = pl.ds(pair * INNER, INNER)
        first, second = fold_rows(total_ref[:, lanes] * gate_ref[:, lanes].astype(F32))
        cotangent_ref[2 * pair] = first.astype(BF16)
        cotangent_ref[2 * pair + 1] = second.astype(BF16)


def project_kernel(order, spot_ref, gated_ref, weight_hbm, *refs):
    out_refs, (buffers, semaphores) = refs[: len(order)], refs[len(order) :]
    depth, side = spot_ref[0], spot_ref[1]

    def column(step):
        layer = lax.rem(depth + order[step // 2], len(order))
        return 2 * layer + (side if step % 2 == 0 else 1 - side)

    def use(step, weight):
        out_refs[step // 2][step % 2] = dot(gated_ref[...], weight[...]).astype(BF16)

    stream_weight(weight_hbm, column, buffers, semaphores, 2 * len(order), use)


def weight_grad_kernel(scale, spot_ref, gated_ref, columns_hbm, far1_hbm, far2_hbm, far3_hbm, out_ref, wide_ref, semaphores):
    count, rows, width = wide_ref.shape
    split = width // 2
    quarter = rows // 4

    @pl.when(pl.program_id(0) == 0)
    def _():
        moves = [(columns_hbm.at[:, pl.ds(0, rows)], wide_ref.at[:, :, pl.ds(0, split)])]
        sources = (columns_hbm.at[:, pl.ds(rows, quarter)], far1_hbm, far2_hbm, far3_hbm)
        for back, source in enumerate(sources):
            layer = lax.rem(spot_ref[0] + 4 - back, 4)
            part = pl.ds(pl.multiple_of(layer * quarter, quarter), quarter)
            moves.append((source, wide_ref.at[:, part, pl.ds(split, split)]))
        for copy in fetch(moves, semaphores):
            copy.wait()

    columns = wide_ref[...].reshape(count * rows, width)
    total = lax.dot_general(gated_ref[...], columns, (((0,), (0,)), ((), ())), preferred_element_type=F32)
    out_ref[...] = (total * scale).astype(BF16)


def shape(dims, kind):
    return jax.ShapeDtypeStruct(dims, kind)


def params(mebibytes=16):
    return pltpu.CompilerParams(vmem_limit_bytes=mebibytes * 1024 * 1024)


def after(array, other):
    return lax.optimization_barrier((array, other))[0]


def exchange(array, axis, groups=None):
    return lax.all_to_all(array, axis, split_axis=0, concat_axis=0, tiled=True, axis_index_groups=groups)


def cost(microseconds):
    return pl.CostEstimate(flops=0, bytes_accessed=int(microseconds * 3.5e6), transcendentals=0)


def body(gate_input, value_input, filter_taps, out_weight, grad_output):
    rows, channels = gate_input.shape
    shards = lax.axis_size("seq")
    groups = lax.axis_size("ch")
    scale = 1.0 / math.sqrt(rows * shards)
    width = channels * groups // shards
    table = jnp.asarray(transform_table(), BF16)
    planes = pltpu.VMEM((2 * BLOCKS, INNER, INNER), BF16)
    spectra = pltpu.VMEM((BLOCKS + 1, 2 * INNER, INNER), BF16)
    anywhere = pl.BlockSpec(memory_space=pl.ANY)
    vmem = pl.BlockSpec(memory_space=pltpu.VMEM)
    smem = pl.BlockSpec(memory_space=pltpu.SMEM)
    place = lax.axis_index("ch")
    ring = groups // 2
    spot = jnp.stack([place // 2, place % 2]).astype(jnp.int32)
    ahead_by = lambda ahead: [(i, (i + 2 * ahead) % groups) for i in range(groups)]
    across = [(i, i ^ 1) for i in range(groups)]
    layers = [[2 * i + j for i in range(ring)] for j in range(2)]

    partner = lax.ppermute(grad_output, "ch", across)
    pair = pl.pallas_call(
        pack_kernel,
        out_shape=shape((shards, rows, INNER), BF16),
        compiler_params=params(60),
        cost_estimate=cost(2),
        name="pack",
    )(value_input, filter_taps)
    partner = after(partner, pair)
    sides = jnp.stack([grad_output, partner])
    grad_full = lax.all_gather(sides, "ch", axis=0, tiled=True, axis_index_groups=layers)
    pair = exchange(pair, "seq")
    packed, spec = pl.pallas_call(
        convolve_kernel,
        out_specs=(vmem, anywhere),
        out_shape=(shape((shards, HALF, INNER), BF16), shape((BLOCKS + 1, 2 * INNER, INNER), BF16)),
        scratch_shapes=[spectra, planes, planes, pltpu.SemaphoreType.DMA],
        compiler_params=params(16),
        cost_estimate=cost(3),
        name="convolve",
    )(pair, table)
    conv, gated = pl.pallas_call(
        gate_kernel,
        out_shape=(shape((rows, channels), F32), shape((rows, channels), BF16)),
        compiler_params=params(),
        cost_estimate=cost(1),
        name="gate",
    )(exchange(packed, "seq"), gate_input)

    gated_all = lax.all_gather(gated, "seq", axis=0, tiled=True)
    split, quarter = width // 2, rows // ring
    columns = pl.pallas_call(
        columns_kernel,
        in_specs=[smem, vmem],
        out_shape=shape((shards, rows + quarter, split), BF16),
        compiler_params=params(60),
        cost_estimate=cost(2),
        name="columns",
    )(spot, grad_full)
    columns = exchange(after(columns, gated), "seq")

    stream_scratch = [pltpu.VMEM((4, channels, channels), BF16), pltpu.SemaphoreType.DMA((4,))]
    pre_grad, cotangent = pl.pallas_call(
        pre_grad_kernel,
        in_specs=[smem, vmem, anywhere, vmem],
        out_shape=(shape((rows, channels), F32), shape((shards, HALF, INNER), BF16)),
        scratch_shapes=stream_scratch,
        compiler_params=params(50),
        cost_estimate=cost(9),
        name="pre_grad",
    )(spot, grad_full, out_weight, gate_input)
    gate_grad = (pre_grad * conv).astype(BF16)

    order = (2, 1, 3, 0)
    parts = pl.pallas_call(
        functools.partial(project_kernel, order),
        in_specs=[smem, vmem, anywhere],
        out_shape=[shape((2, rows, channels), BF16)] * ring,
        scratch_shapes=stream_scratch,
        compiler_params=params(50),
        cost_estimate=cost(8),
        name="project",
    )(spot, gated, out_weight)
    parts = [lax.ppermute(part, "ch", ahead_by(ahead)) if ahead else part for part, ahead in zip(parts, order)]

    part = columns[:, rows:]
    shared = [lax.ppermute(part, "ch", ahead_by(ahead)) for ahead in (1, 2, 3)]
    parts = [after(got, (columns, cotangent)) for got in parts]
    cotangent = exchange(after(cotangent, (columns, gate_grad)), "seq")
    returned = pl.pallas_call(
        correlate_kernel,
        out_shape=shape((shards, rows, INNER), BF16),
        in_specs=[vmem, anywhere, vmem],
        scratch_shapes=[spectra, pltpu.VMEM((shards, rows, INNER), BF16), planes, planes, pltpu.SemaphoreType.DMA],
        compiler_params=params(16),
        cost_estimate=cost(3),
        name="correlate",
    )(after(cotangent, tuple(parts)), spec, table)

    parts = [after(got, returned) for got in parts]
    opposite = sum(part[1].astype(F32) for part in parts).astype(BF16)
    kept = sum(part[0].astype(F32) for part in parts)
    returned = exchange(returned, "seq")

    opposite = lax.ppermute(opposite, "ch", across)

    weight_grad = pl.pallas_call(
        functools.partial(weight_grad_kernel, scale),
        grid=(4,),
        in_specs=[smem, pl.BlockSpec((shards * rows, channels // 4), lambda step: (0, step))] + [anywhere] * ring,
        out_specs=pl.BlockSpec((channels // 4, width), lambda step: (step, 0)),
        out_shape=shape((channels, width), BF16),
        scratch_shapes=[pltpu.VMEM((shards, rows, width), BF16), pltpu.SemaphoreType.DMA((ring + 1,))],
        compiler_params=params(60),
        cost_estimate=cost(6),
        name="weight_grad",
    )(spot, gated_all, columns, *shared)
    value_grad, filter_grad = pl.pallas_call(
        functools.partial(finish_kernel, scale),
        out_shape=(shape((rows, channels), BF16), shape((rows, channels), F32)),
        compiler_params=params(),
        cost_estimate=cost(1),
        name="finish",
    )(after(returned, weight_grad))
    opposite = after(opposite, weight_grad)
    block_output = (kept + opposite.astype(F32)).astype(BF16)
    return (block_output, gate_grad, value_grad, filter_grad, weight_grad)


def solution(mesh):
    placed = (P("seq", "ch"), P("seq", "ch"), P("seq", "ch"), P("ch", None), P("seq", "ch"))
    return jax.shard_map(
        body,
        mesh=mesh,
        in_specs=placed,
        out_specs=(P("seq", "ch"), P("seq", "ch"), P("seq", "ch"), P("seq", "ch"), P("ch", "seq")),
        check_vma=False,
    )
```

time: 225 us -> 136 us (0.60)
  blocking collectives: 124 us -> 27.5 us
  starting transfers between devices: 11.7 us -> 29.1 us
  waiting for transfers between devices: 23.1 us -> 14.3 us
  matrix products: 6.2 us -> 0 us
  Pallas kernels: 31.8 us -> 37.7 us
  local copies, waits for them, and re-layouts: 9.82 us -> 5.47 us
  other arithmetic: 3.49 us -> 6.5 us
    all_to_all x5 -> x2, blocking collectives: 124 us -> 27.5 us  [exchange(): lax.all_to_all(array, axis, split_axis=0, concat_axis=0, tiled=True, axis...]
    all_to_all x2 -> x3, waiting for transfers between devices: 23.1 us -> 6.71 us  [exchange(): lax.all_to_all(array, axis, split_axis=0, concat_axis=0, tiled=True, axis...]
    ppermute x0 -> x8, starting transfers between devices: none -> 13.6 us  [the longest x3 4.83 us: body(): lax.ppermute(part, 'ch', ahead_by(ahead))]
    ppermute x0 -> x8, waiting for transfers between devices: none -> 6.96 us  [the longest x1 3.84 us: body(): partner = lax.ppermute(grad_output, 'ch', across)]
    dot_general x1 -> x0, matrix products: 6.2 us -> none  [body(): lax.dot_general(gated_all, columns, (((0,), (0,)), ((), ())), preferred_e...]
    unnamed x32 -> x18, local copies, waits for them, and re-layouts: 8.61 us -> 3.78 us
    pallas_call x3 -> x5, Pallas kernels: 25.1 us -> 29.8 us  [the longest x1 8.61 us: body(): pl.pallas_call(functools.partial(project_kernel, order), in_specs=[smem,...]
    all_to_all x2 -> x3, starting transfers between devices: 11.7 us -> 15.4 us  [exchange(): lax.all_to_all(array, axis, split_axis=0, concat_axis=0, tiled=True, axis...]
  transfers between devices with their start and end apart: 3 -> 13, of which waited for: 1 -> 6; matrix products, arithmetic and copies ran while one was open for 2% -> 3% of each run, Pallas kernels for 12% -> 28%
where the time goes in v2:
time: 136 us; the launch traced here: 135 us
  Pallas kernels  37.7 us (28%)
  starting transfers between devices  29.1 us (21%)
  blocking collectives  27.5 us (20%)
  waiting for transfers between devices  14.3 us (11%)
  between operations  14.2 us (10%)
  other arithmetic  6.5 us (5%)
  local copies, waits for them, and re-layouts  5.47 us (4%)
    all_to_all x2, blocking collectives, exchange(): lax.all_to_all(array, axis, split_axis=0, concat_axis=0, tiled=True, axis...  27.5 us
    all_to_all x3, starting transfers between devices, exchange(): lax.all_to_all(array, axis, split_axis=0, concat_axis=0, tiled=True, axis...  15.4 us
    pallas_call x1, Pallas kernels, body(): pl.pallas_call(functools.partial(project_kernel, order), in_specs=[smem,...  8.61 us
    pallas_call x1, Pallas kernels, body(): pl.pallas_call(pre_grad_kernel, in_specs=[smem, vmem, anywhere, vmem], ou...  8.03 us
    pallas_call x1, Pallas kernels, body(): pl.pallas_call(functools.partial(weight_grad_kernel, scale), grid=(4,), i...  7.35 us
    all_to_all x3, waiting for transfers between devices, exchange(): lax.all_to_all(array, axis, split_axis=0, concat_axis=0, tiled=True, axis...  6.71 us
    ppermute x3, starting transfers between devices, body(): lax.ppermute(part, 'ch', ahead_by(ahead))  4.83 us
    pallas_call x1, Pallas kernels, body(): pl.pallas_call(correlate_kernel, out_shape=shape((shards, rows, INNER), B...  3.86 us
  transfers between devices with their start and end apart: 13, of which 6 were waited for; matrix products, arithmetic and copies ran while one was open for 3% of the time, Pallas kernels for 28%

profile of v2, /device:TPU:1, one launch (start us, length us, event | category | flops | bytes accessed | tf_op | source)
XLA Modules:
  0.0 134.9 jit_solution(1059722154673823785)
XLA Ops:
  7.2 0.0 copy-start
  7.2 0.0 all-gather.3.cloned.1.call-start
  7.2 3.8 %collective-permute-start.1 = (bf16[128,1024]{1,0:T(8,128)(2,1)}, bf16[128,1024]{1,0:T(8,128)(2,1)S(1)}, u32[]{:S(2)}, u32[]{:S(2)}) collective-permute-start(bf16[128,1024]{1,0:T(8,128)(2,1)} %param.10), channel_id=1, source_target_pairs={{0,1},{1,0},{2,3},{3,2},{4,5},{5,4},{6,7},{7,6},{8,9},{9,8},{10,11... | collective-permute-start | bytes 786440 | tf_op jit(solution)/shard_map/ppermute | solution.py:314
  11.0 2.1 %pack.1 = bf16[16,128,128]{2,1,0:T(8,128)(2,1)} custom-call(bf16[128,1024]{1,0:T(8,128)(2,1)} %value_ref.1, f32[128,1024]{1,0:T(8,128)} %taps_ref.1), custom_call_target="tpu_custom_call" | custom-call | bytes 7000000 | tf_op jit(solution)/shard_map/pack/pallas_call | solution.py:315
  13.2 3.8 %collective-permute-done.1 = bf16[128,1024]{1,0:T(8,128)(2,1)S(1)} collective-permute-done((bf16[128,1024]{1,0:T(8,128)(2,1)}, bf16[128,1024]{1,0:T(8,128)(2,1)S(1)}, u32[]{:S(2)}, u32[]{:S(2)}) %collective-permute-start.1) | collective-permute-done | bytes 262176 | tf_op jit(solution)/shard_map/ppermute | solution.py:314
  17.0 1.8 %pad_maximum_fusion = bf16[2,128,1024]{2,1,0:T(8,128)(2,1)} fusion(bf16[1,128,1024]{2,1,0:T(8,128)(2,1)S(1)} %bitcast.11, bf16[1,128,1024]{2,1,0:T(8,128)(2,1)} %bitcast.10), kind=kLoop, calls=%fused_computation | loop fusion | flops 262144 | bytes 1048576 | tf_op jit(solution)/shard_map/stack | solution.py:323
  18.8 0.0 all-gather.3.cloned.1.call-update
  18.8 0.0 all-gather.5.cloned.1.call-start
  18.9 16.8 %all_to_all.25.pair_ref = bf16[16,128,128]{2,1,0:T(8,128)(2,1)S(1)} all-to-all(bf16[16,128,128]{2,1,0:T(8,128)(2,1)} %pack.1), channel_id=1, replica_groups=mesh['seq'=16,'ch'=8] {'seq'}, dimensions={0} | all-to-all | bytes 1048576 | tf_op jit(solution)/shard_map/all_to_all | solution.py:288
  35.6 0.0 copy-done
  35.7 0.0 copy-start.4
  35.7 2.9 %convolve.1 = (bf16[16,64,128]{2,1,0:T(8,128)(2,1)S(1)}, bf16[17,256,128]{2,1,0:T(8,128)(2,1)S(1)}) custom-call(bf16[16,128,128]{2,1,0:T(8,128)(2,1)S(1)} %all_to_all.25.pair_ref, bf16[42,256,128]{2,1,0:T(8,128)(2,1)S(1)} %copy-done), custom_call_target="tpu_custom_call" | custom-call | bytes 10500000 | tf_op jit(solution)/shard_map/convolve/pallas_call | solution.py:326
  38.6 0.0 copy-start.2
  38.6 1.0 copy-done.2
  39.6 10.7 %all_to_all.26.recv_ref = bf16[16,64,128]{2,1,0:T(8,128)(2,1)S(1)} all-to-all(bf16[16,64,128]{2,1,0:T(8,128)(2,1)S(1)} %get-tuple-element.31), channel_id=1, replica_groups=mesh['seq'=16,'ch'=8] {'seq'}, dimensions={0} | all-to-all | bytes 524288 | tf_op jit(solution)/shard_map/all_to_all | solution.py:288
  50.3 0.0 copy-done.4
  50.3 0.9 gate.1
  51.2 0.0 copy-start.5
  51.2 0.8 copy-done.5
  52.0 0.0 all-gather.5.cloned.1.call-update
  52.0 0.6 pad_add_fusion.spot_ref
  52.7 0.6 all-gather.3.cloned.1.call-done.grad_ref
  53.3 2.8 %columns.1 = bf16[16,160,256]{2,1,0:T(8,128)(2,1)} custom-call(s32[2]{0:T(128)} %pad_add_fusion.spot_ref, bf16[8,128,1024]{2,1,0:T(8,128)(2,1)} %all-gather.3.cloned.1.call-done.grad_ref), custom_call_target="tpu_custom_call" | custom-call | bytes 7000000 | tf_op jit(solution)/shard_map/columns/pallas_call | solution.py:345
  56.1 0.0 copy-start.8
  56.1 6.0 %all-to-all-start.2 = ((bf16[16,160,256]{2,1,0:T(8,128)(2,1)}), bf16[16,160,256]{2,1,0:T(8,128)(2,1)}, u32[]{:S(2)}, u32[]{:S(2)}) async-start(bf16[16,160,256]{2,1,0:T(8,128)(2,1)} %columns.1), calls=%async_computation.2 | async-start | bytes 2621440 | tf_op jit(solution)/shard_map/all_to_all | solution.py:288
  62.1 0.0 copy-done.8
  62.1 0.0 copy-start.1
  62.2 8.6 %project.1 = (bf16[2,128,1024]{2,1,0:T(8,128)(2,1)}, bf16[2,128,1024]{2,1,0:T(8,128)(2,1)}, bf16[2,128,1024]{2,1,0:T(8,128)(2,1)}, bf16[2,128,1024]{2,1,0:T(8,128)(2,1)S(1)}) custom-call(s32[2]{0:T(128)S(1)} %copy-done.8, bf16[128,1024]{1,0:T(8,128)(2,1)} %get-tuple-element.32.gated_ref, bf16[1024,8192]{1,0:T(8,128)(2,1)} %weight_hbm.3), custom_call_target="tpu_custom_call" | custom-call | bytes 28000000 | tf_op jit(solution)/shard_map/project/pallas_call | solution.py:368
  70.8 2.2 %collective-permute-start = (bf16[2,128,1024]{2,1,0:T(8,128)(2,1)}, bf16[2,128,1024]{2,1,0:T(8,128)(2,1)}, u32[]{:S(2)}, u32[]{:S(2)}) collective-permute-start(bf16[2,128,1024]{2,1,0:T(8,128)(2,1)} %get-tuple-element.33), channel_id=1, source_target_pairs={{0,4},{1,5},{2,6},{3,7},{4,0},{5,1},{6,2},{7,3},{8,12},{9,13},{10,... | collective-permute-start | bytes 1572872 | tf_op jit(solution)/shard_map/ppermute | solution.py:377
  72.9 0.7 collective-permute-start.2
  73.6 0.0 copy-start.6
  73.6 2.0 %collective-permute-start.3 = (bf16[2,128,1024]{2,1,0:T(8,128)(2,1)}, bf16[2,128,1024]{2,1,0:T(8,128)(2,1)}, u32[]{:S(2)}, u32[]{:S(2)}) collective-permute-start(bf16[2,128,1024]{2,1,0:T(8,128)(2,1)} %get-tuple-element.43), channel_id=1, source_target_pairs={{0,6},{1,7},{2,0},{3,1},{4,2},{5,3},{6,4},{7,5},{8,14},{9,15},{10,... | collective-permute-start | bytes 1572872 | tf_op jit(solution)/shard_map/ppermute | solution.py:377
  75.6 0.0 copy-done.1
  75.6 8.0 %pre_grad.1 = (f32[128,1024]{1,0:T(8,128)S(1)}, bf16[16,64,128]{2,1,0:T(8,128)(2,1)S(1)}) custom-call(s32[2]{0:T(128)S(1)} %copy-done.8, bf16[8,128,1024]{2,1,0:T(8,128)(2,1)S(1)} %copy-done.1, bf16[1024,8192]{1,0:T(8,128)(2,1)} %weight_hbm.3, bf16[128,1024]{1,0:T(8,128)(2,1)S(1)} %copy-done.4), custom_call_target="tpu_custom_call" | custom-call | bytes 31500000 | tf_op jit(solution)/shard_map/pre_grad/pallas_call | solution.py:356
  83.7 0.0 copy-start.7
  83.7 0.7 copy-done.7
  84.4 0.0 copy-done.6
  84.4 0.8 multiply_convert_fusion
  85.1 2.1 %all-to-all-done.2.columns_hbm = bf16[16,160,256]{2,1,0:T(8,128)(2,1)} async-done(((bf16[16,160,256]{2,1,0:T(8,128)(2,1)}), bf16[16,160,256]{2,1,0:T(8,128)(2,1)}, u32[]{:S(2)}, u32[]{:S(2)}) %all-to-all-start.2) | async-done | bytes 1310752 | tf_op jit(solution)/shard_map/all_to_all | solution.py:288
  87.2 5.8 %all-to-all-start.3 = ((bf16[16,64,128]{2,1,0:T(8,128)(2,1)}), bf16[16,64,128]{2,1,0:T(8,128)(2,1)S(1)}, u32[]{:S(2)}, u32[]{:S(2)}) async-start(bf16[16,64,128]{2,1,0:T(8,128)(2,1)} %copy-done.7), calls=%async_computation.3 | async-start | bytes 524288 | tf_op jit(solution)/shard_map/all_to_all | solution.py:288
  93.0 1.7 %slice.36 = bf16[16,32,256]{2,1,0:T(8,128)(2,1)} slice(bf16[16,160,256]{2,1,0:T(8,128)(2,1)} %all-to-all-done.2.columns_hbm), slice={[0:16], [128:160], [0:256]} | slice | bytes 524288 | tf_op jit(solution)/shard_map/slice | solution.py:379
  94.7 2.0 %collective-permute-start.7 = (bf16[16,32,256]{2,1,0:T(8,128)(2,1)}, bf16[16,32,256]{2,1,0:T(8,128)(2,1)}, u32[]{:S(2)}, u32[]{:S(2)}) collective-permute-start(bf16[16,32,256]{2,1,0:T(8,128)(2,1)} %slice.36), channel_id=1, source_target_pairs={{0,6},{1,7},{2,0},{3,1},{4,2},{5,3},{6,4},{7,5},{8,14},{9,15},{10,... | collective-permute-start | bytes 786440 | tf_op jit(solution)/shard_map/ppermute | solution.py:380
  96.6 0.0 collective-permute-start.6
  96.6 0.0 collective-permute-done
  96.6 0.7 collective-permute-start.5
  97.3 0.4 collective-permute-done.2
  97.8 0.0 collective-permute-done.3
  97.8 4.6 %all-to-all-done.3.grad_ref = bf16[16,64,128]{2,1,0:T(8,128)(2,1)S(1)} async-done(((bf16[16,64,128]{2,1,0:T(8,128)(2,1)}), bf16[16,64,128]{2,1,0:T(8,128)(2,1)S(1)}, u32[]{:S(2)}, u32[]{:S(2)}) %all-to-all-start.3) | async-done | bytes 262176 | tf_op jit(solution)/shard_map/all_to_all | solution.py:288
  102.4 0.0 copy-start.3
  102.4 1.3 copy-done.3
  103.7 3.9 %correlate.1 = bf16[16,128,128]{2,1,0:T(8,128)(2,1)} custom-call(bf16[16,64,128]{2,1,0:T(8,128)(2,1)S(1)} %all-to-all-done.3.grad_ref, bf16[17,256,128]{2,1,0:T(8,128)(2,1)S(1)} %copy-done.3, bf16[42,256,128]{2,1,0:T(8,128)(2,1)S(1)} %copy-done), custom_call_target="tpu_custom_call" | custom-call | bytes 10500000 | tf_op jit(solution)/shard_map/correlate/pallas_call | solution.py:383
  107.5 3.7 %all-to-all-start.4 = ((bf16[16,128,128]{2,1,0:T(8,128)(2,1)}), bf16[16,128,128]{2,1,0:T(8,128)(2,1)S(1)}, u32[]{:S(2)}, u32[]{:S(2)}) async-start(bf16[16,128,128]{2,1,0:T(8,128)(2,1)} %correlate.1), calls=%async_computation.4 | async-start | bytes 1048576 | tf_op jit(solution)/shard_map/all_to_all | solution.py:288
  111.2 1.3 fusion.1
  112.5 2.3 %collective-permute-start.4 = (bf16[128,1024]{1,0:T(8,128)(2,1)S(1)}, bf16[128,1024]{1,0:T(8,128)(2,1)S(1)}, u32[]{:S(2)}, u32[]{:S(2)}) collective-permute-start(bf16[128,1024]{1,0:T(8,128)(2,1)S(1)} %fusion.1), channel_id=1, source_target_pairs={{0,1},{1,0},{2,3},{3,2},{4,5},{5,4},{6,7},{7,6},{8,9},{9,8},{10,11... | collective-permute-start | bytes 786440 | tf_op jit(solution)/shard_map/ppermute | solution.py:398
  114.8 0.0 collective-permute-done.7.far3_hbm
  114.8 0.0 collective-permute-done.6.far2_hbm
  114.8 0.0 collective-permute-done.5.far1_hbm
  114.8 0.0 all-gather.5.cloned.1.call-done.gated_ref
  114.8 7.4 %weight_grad.1 = bf16[1024,512]{1,0:T(8,128)(2,1)} custom-call(s32[2]{0:T(128)} %pad_add_fusion.spot_ref, bf16[2048,1024]{1,0:T(8,128)(2,1)} %all-gather.5.cloned.1.call-done.gated_ref, bf16[16,160,256]{2,1,0:T(8,128)(2,1)} %all-to-all-done.2.columns_hbm, bf16[16,32,256]{2,1,0:T(8,128)(2,1)} %collective-permute-done.5.far1_hbm, ...), custom_call_target="tpu_custom_call" | custom-call | bytes 21000000 | tf_op jit(solution)/shard_map/weight_grad/pallas_call | solution.py:400
  122.2 0.0 all-to-all-done.4.recv_ref
  122.2 1.1 finish.1
  123.3 2.7 %collective-permute-done.4 = bf16[128,1024]{1,0:T(8,128)(2,1)S(1)} collective-permute-done((bf16[128,1024]{1,0:T(8,128)(2,1)S(1)}, bf16[128,1024]{1,0:T(8,128)(2,1)S(1)}, u32[]{:S(2)}, u32[]{:S(2)}) %collective-permute-start.4) | collective-permute-done | bytes 262176 | tf_op jit(solution)/shard_map/ppermute | solution.py:398
  126.0 2.0 %fusion = bf16[128,1024]{1,0:T(8,128)(2,1)} fusion(bf16[128,1024]{1,0:T(8,128)(2,1)S(1)} %collective-permute-done.4, bf16[2,128,1024]{2,1,0:T(8,128)(2,1)S(1)} %get-tuple-element.52, bf16[2,128,1024]{2,1,0:T(8,128)(2,1)} %collective-permute-done.3, bf16[2,128,1024]{2,1,0:T(8,128)(2,1)} %collective-permute-done.2, bf16[2,128,1024]{2,1,0:T(8,128)(2,1)} %collective-permute-done), kind=kLoop, calls=%fused_computation.2 | loop fusion | flops 1310720 | bytes 1572864 | tf_op jit(solution)/shard_map/convert_element_type | solution.py:419
Async XLA Ops:
  7.2 28.5 %copy-start = (bf16[42,256,128]{2,1,0:T(8,128)(2,1)S(1)}, bf16[42,256,128]{2,1,0:T(8,128)(2,1)}, u32[]{:S(2)}) copy-start(bf16[42,256,128]{2,1,0:T(8,128)(2,1)} %constant.30.clone.table_ref) | copy-start | bytes 8257540
  7.2 46.1 %all-gather.3.cloned.1.call-start = ((), (), s32[]{:S(2)}) async-start(), calls=%async_computation.5 | async-start | bytes 2621440 | tf_op jit(solution)/shard_map/all_gather | solution.py:324
  7.2 9.8 %collective-permute-start.1 = (bf16[128,1024]{1,0:T(8,128)(2,1)}, bf16[128,1024]{1,0:T(8,128)(2,1)S(1)}, u32[]{:S(2)}, u32[]{:S(2)}) collective-permute-start(bf16[128,1024]{1,0:T(8,128)(2,1)} %param.10), channel_id=1, source_target_pairs={{0,1},{1,0},{2,3},{3,2},{4,5},{5,4},{6,7},{7,6},{8,9},{9,8},{10,11... | collective-permute-start | bytes 786440 | tf_op jit(solution)/shard_map/ppermute | solution.py:314
  18.8 96.0 %all-gather.5.cloned.1.call-start = ((), (), s32[]{:S(2)}) async-start(), calls=%async_computation.6 | async-start | bytes 4456448 | tf_op jit(solution)/shard_map/all_gather | solution.py:343
  35.7 14.6 %copy-start.4 = (bf16[128,1024]{1,0:T(8,128)(2,1)S(1)}, bf16[128,1024]{1,0:T(8,128)(2,1)}, u32[]{:S(2)}) copy-start(bf16[128,1024]{1,0:T(8,128)(2,1)} %gate_ref.3) | copy-start | bytes 786436
  38.6 1.0 copy-start.2
  51.2 0.8 copy-start.5
  56.1 6.0 %copy-start.8 = (s32[2]{0:T(128)S(1)}, s32[2]{0:T(128)}, u32[]{:S(2)}) copy-start(s32[2]{0:T(128)} %pad_add_fusion.spot_ref) | copy-start | bytes 28
  56.1 31.1 %all-to-all-start.2 = ((bf16[16,160,256]{2,1,0:T(8,128)(2,1)}), bf16[16,160,256]{2,1,0:T(8,128)(2,1)}, u32[]{:S(2)}, u32[]{:S(2)}) async-start(bf16[16,160,256]{2,1,0:T(8,128)(2,1)} %columns.1), calls=%async_computation.2 | async-start | bytes 2621440 | tf_op jit(solution)/shard_map/all_to_all | solution.py:288
  62.1 13.5 %copy-start.1 = (bf16[8,128,1024]{2,1,0:T(8,128)(2,1)S(1)}, bf16[8,128,1024]{2,1,0:T(8,128)(2,1)}, u32[]{:S(2)}) copy-start(bf16[8,128,1024]{2,1,0:T(8,128)(2,1)} %all-gather.3.cloned.1.call-done.grad_ref) | copy-start | bytes 6291460
  70.8 25.9 %collective-permute-start = (bf16[2,128,1024]{2,1,0:T(8,128)(2,1)}, bf16[2,128,1024]{2,1,0:T(8,128)(2,1)}, u32[]{:S(2)}, u32[]{:S(2)}) collective-permute-start(bf16[2,128,1024]{2,1,0:T(8,128)(2,1)} %get-tuple-element.33), channel_id=1, source_target_pairs={{0,4},{1,5},{2,6},{3,7},{4,0},{5,1},{6,2},{7,3},{8,12},{9,13},{10,... | collective-permute-start | bytes 1572872 | tf_op jit(solution)/shard_map/ppermute | solution.py:377
  72.9 24.8 %collective-permute-start.2 = (bf16[2,128,1024]{2,1,0:T(8,128)(2,1)}, bf16[2,128,1024]{2,1,0:T(8,128)(2,1)}, u32[]{:S(2)}, u32[]{:S(2)}) collective-permute-start(bf16[2,128,1024]{2,1,0:T(8,128)(2,1)} %get-tuple-element.41), channel_id=1, source_target_pairs={{0,2},{1,3},{2,4},{3,5},{4,6},{5,7},{6,0},{7,1},{8,10},{9,11},{10,... | collective-permute-start | bytes 1572872 | tf_op jit(solution)/shard_map/ppermute | solution.py:377
  73.6 10.7 %copy-start.6 = (f32[128,1024]{1,0:T(8,128)S(1)}, f32[128,1024]{1,0:T(8,128)}, u32[]{:S(2)}) copy-start(f32[128,1024]{1,0:T(8,128)} %copy-done.5) | copy-start | bytes 1572868
  73.6 24.1 %collective-permute-start.3 = (bf16[2,128,1024]{2,1,0:T(8,128)(2,1)}, bf16[2,128,1024]{2,1,0:T(8,128)(2,1)}, u32[]{:S(2)}, u32[]{:S(2)}) collective-permute-start(bf16[2,128,1024]{2,1,0:T(8,128)(2,1)} %get-tuple-element.43), channel_id=1, source_target_pairs={{0,6},{1,7},{2,0},{3,1},{4,2},{5,3},{6,4},{7,5},{8,14},{9,15},{10,... | collective-permute-start | bytes 1572872 | tf_op jit(solution)/shard_map/ppermute | solution.py:377
  83.7 0.7 copy-start.7
  87.2 15.2 %all-to-all-start.3 = ((bf16[16,64,128]{2,1,0:T(8,128)(2,1)}), bf16[16,64,128]{2,1,0:T(8,128)(2,1)S(1)}, u32[]{:S(2)}, u32[]{:S(2)}) async-start(bf16[16,64,128]{2,1,0:T(8,128)(2,1)} %copy-done.7), calls=%async_computation.3 | async-start | bytes 524288 | tf_op jit(solution)/shard_map/all_to_all | solution.py:288
  94.7 20.1 %collective-permute-start.7 = (bf16[16,32,256]{2,1,0:T(8,128)(2,1)}, bf16[16,32,256]{2,1,0:T(8,128)(2,1)}, u32[]{:S(2)}, u32[]{:S(2)}) collective-permute-start(bf16[16,32,256]{2,1,0:T(8,128)(2,1)} %slice.36), channel_id=1, source_target_pairs={{0,6},{1,7},{2,0},{3,1},{4,2},{5,3},{6,4},{7,5},{8,14},{9,15},{10,... | collective-permute-start | bytes 786440 | tf_op jit(solution)/shard_map/ppermute | solution.py:380
  96.6 18.2 %collective-permute-start.6 = (bf16[16,32,256]{2,1,0:T(8,128)(2,1)}, bf16[16,32,256]{2,1,0:T(8,128)(2,1)}, u32[]{:S(2)}, u32[]{:S(2)}) collective-permute-start(bf16[16,32,256]{2,1,0:T(8,128)(2,1)} %slice.36), channel_id=1, source_target_pairs={{0,4},{1,5},{2,6},{3,7},{4,0},{5,1},{6,2},{7,3},{8,12},{9,13},{10,... | collective-permute-start | bytes 786440 | tf_op jit(solution)/shard_map/ppermute | solution.py:380
  96.6 18.2 %collective-permute-start.5 = (bf16[16,32,256]{2,1,0:T(8,128)(2,1)}, bf16[16,32,256]{2,1,0:T(8,128)(2,1)}, u32[]{:S(2)}, u32[]{:S(2)}) collective-permute-start(bf16[16,32,256]{2,1,0:T(8,128)(2,1)} %slice.36), channel_id=1, source_target_pairs={{0,2},{1,3},{2,4},{3,5},{4,6},{5,7},{6,0},{7,1},{8,10},{9,11},{10,... | collective-permute-start | bytes 786440 | tf_op jit(solution)/shard_map/ppermute | solution.py:380
  102.4 1.3 copy-start.3
  107.5 14.7 %all-to-all-start.4 = ((bf16[16,128,128]{2,1,0:T(8,128)(2,1)}), bf16[16,128,128]{2,1,0:T(8,128)(2,1)S(1)}, u32[]{:S(2)}, u32[]{:S(2)}) async-start(bf16[16,128,128]{2,1,0:T(8,128)(2,1)} %correlate.1), calls=%async_computation.4 | async-start | bytes 1048576 | tf_op jit(solution)/shard_map/all_to_all | solution.py:288
  112.5 13.5 %collective-permute-start.4 = (bf16[128,1024]{1,0:T(8,128)(2,1)S(1)}, bf16[128,1024]{1,0:T(8,128)(2,1)S(1)}, u32[]{:S(2)}, u32[]{:S(2)}) collective-permute-start(bf16[128,1024]{1,0:T(8,128)(2,1)S(1)} %fusion.1), channel_id=1, source_target_pairs={{0,1},{1,0},{2,3},{3,2},{4,5},{5,4},{6,7},{7,6},{8,9},{9,8},{10,11... | collective-permute-start | bytes 786440 | tf_op jit(solution)/shard_map/ppermute | solution.py:398
Sparse Core Ops, SparseCore 0:
  18.9 34.3 all-gather.2
  55.6 50.3 all-gather.4

commit v3 on v2

--- a/solution.py
+++ b/solution.py
@@ -172,12 +172,12 @@
     return copies
 
 
-def gate_kernel(recv_ref, gate_ref, conv_ref, gated_ref):
+def gate_kernel(recv_ref, gate_ref, pre_ref, gated_ref, gate_grad_ref):
     for pair in range(BLOCKS // 2):
         conv = unfold_rows(recv_ref[2 * pair].astype(F32), recv_ref[2 * pair + 1].astype(F32))
         lanes = pl.ds(pair * INNER, INNER)
-        conv_ref[:, lanes] = conv
         gated_ref[:, lanes] = (gate_ref[:, lanes].astype(F32) * conv).astype(BF16)
+        gate_grad_ref[:, lanes] = (pre_ref[:, lanes] * conv).astype(BF16)
 
 
 def finish_kernel(scale, recv_ref, value_grad_ref, filter_grad_ref):
@@ -206,35 +206,46 @@
         use(step, buffers.at[step % depth])
 
 
-def grad_column(spot_ref, block):
-    return block // 2 * 2 + lax.rem(spot_ref[1] + block % 2, 2)
-
-
-def columns_kernel(spot_ref, grad_ref, out_ref):
-    blocks, rows, channels = grad_ref.shape
-    split = channels // 4
-    quarter = rows // 4
-    part = pl.ds(pl.multiple_of(spot_ref[0] * quarter, quarter), quarter)
-    for block in range(blocks):
+DIRECT = 1
+
+
+def column_rows(piece):
+    if piece < DIRECT:
+        return HALF + piece * INNER, INNER
+    return HALF + DIRECT * INNER + (piece - DIRECT) * HALF, HALF
+
+
+def gathered_block(spot_ref, step):
+    depth, side = spot_ref[0], spot_ref[1]
+    if step < 4:
+        return 2 * step + side
+    return 2 * lax.rem(depth + 8 - step, 4) + 1 - side
+
+
+def pre_grad_kernel(spot_ref, near_ref, far0_ref, far1_ref, far2_ref, far3_ref, weight_hbm, gate_ref, *refs):
+    total_ref, send_ref, buffers, semaphores = refs
+    ring, rows, channels = near_ref.shape
+    far = (far0_ref, far1_ref, far2_ref, far3_ref)
+    upper = pl.ds(pl.multiple_of(lax.rem(spot_ref[0], 2) * HALF, HALF), HALF)
+
+    def use(step, weight):
+        block_ref = near_ref.at[step] if step < ring else far[step - ring]
+        part = lax.dot_general(block_ref[...], weight[...], (((1,), (1,)), ((), ())), preferred_element_type=F32)
+        total_ref[...] = part if step == 0 else total_ref[...] + part
         for half in range(2):
-            target = 2 * grad_column(spot_ref, block) + half
-            start = 2 * half * split
-            out_ref[target, :rows] = grad_ref[block, :, start : start + split]
-            out_ref[target, rows:] = grad_ref[block, part, start + split : start + 2 * split]
-
-
-def pre_grad_kernel(spot_ref, grad_ref, weight_hbm, gate_ref, total_ref, cotangent_ref, buffers, semaphores):
-    def use(step, weight):
-        part = lax.dot_general(grad_ref[step], weight[...], (((1,), (1,)), ((), ())), preferred_element_type=F32)
-        total_ref[...] = part if step == 0 else total_ref[...] + part
-
-    column = functools.partial(grad_column, spot_ref)
-    stream_weight(weight_hbm, column, buffers, semaphores, grad_ref.shape[0], use)
+            target = 2 * gathered_block(spot_ref, step) + half
+            start = half * (channels // 2)
+            for piece in range(4):
+                lanes = pl.ds(start + piece * INNER, INNER)
+                place, size = column_rows(piece)
+                send_ref[target, pl.ds(place, size)] = block_ref[:, lanes] if piece < DIRECT else block_ref[upper, lanes]
+
+    stream_weight(weight_hbm, functools.partial(gathered_block, spot_ref), buffers, semaphores, 2 * ring, use)
     for pair in range(BLOCKS // 2):
         lanes = pl.ds(pair * INNER, INNER)
         first, second = fold_rows(total_ref[:, lanes] * gate_ref[:, lanes].astype(F32))
-        cotangent_ref[2 * pair] = first.astype(BF16)
-        cotangent_ref[2 * pair + 1] = second.astype(BF16)
+        send_ref[2 * pair, :HALF] = first.astype(BF16)
+        send_ref[2 * pair + 1, :HALF] = second.astype(BF16)
 
 
 def project_kernel(order, spot_ref, gated_ref, weight_hbm, *refs):
@@ -251,25 +262,46 @@
     stream_weight(weight_hbm, column, buffers, semaphores, 2 * len(order), use)
 
 
-def weight_grad_kernel(scale, spot_ref, gated_ref, columns_hbm, far1_hbm, far2_hbm, far3_hbm, out_ref, wide_ref, semaphores):
+def weight_grad_kernel(scale, spot_ref, gated_hbm, received_hbm, shared_hbm, out_ref, gated_ref, wide_ref, total_ref, arrived, semaphores):
+    parts = gated_ref.shape[0]
+    side = lax.rem(spot_ref[0], 2)
+    own = pl.ds(pl.multiple_of(side * HALF, HALF), HALF)
+    other = pl.ds(pl.multiple_of((1 - side) * HALF, HALF), HALF)
+    moves = []
+    for piece in range(4):
+        lanes = pl.ds(piece * INNER, INNER)
+        place, size = column_rows(piece)
+        source = received_hbm.at[:, pl.ds(place, size)]
+        if piece < DIRECT:
+            moves.append((source, wide_ref.at[:, :, lanes]))
+        else:
+            moves.append((source, wide_ref.at[:, own, lanes]))
+            part = pl.ds((piece - DIRECT) * HALF, HALF)
+            moves.append((shared_hbm.at[:, part], wide_ref.at[:, other, lanes]))
+    copies = fetch(moves, semaphores)
+    loads = fetch([(gated_hbm.at[part], gated_ref.at[part]) for part in range(parts)], arrived)
+    for copy in copies:
+        copy.wait()
     count, rows, width = wide_ref.shape
-    split = width // 2
-    quarter = rows // 4
-
-    @pl.when(pl.program_id(0) == 0)
-    def _():
-        moves = [(columns_hbm.at[:, pl.ds(0, rows)], wide_ref.at[:, :, pl.ds(0, split)])]
-        sources = (columns_hbm.at[:, pl.ds(rows, quarter)], far1_hbm, far2_hbm, far3_hbm)
-        for back, source in enumerate(sources):
-            layer = lax.rem(spot_ref[0] + 4 - back, 4)
-            part = pl.ds(pl.multiple_of(layer * quarter, quarter), quarter)
-            moves.append((source, wide_ref.at[:, part, pl.ds(split, split)]))
-        for copy in fetch(moves, semaphores):
-            copy.wait()
-
-    columns = wide_ref[...].reshape(count * rows, width)
-    total = lax.dot_general(gated_ref[...], columns, (((0,), (0,)), ((), ())), preferred_element_type=F32)
-    out_ref[...] = (total * scale).astype(BF16)
+    tile = out_ref.shape[0] // 4
+    for part in range(parts):
+        loads[part].wait()
+        columns = wide_ref[part * count // parts : (part + 1) * count // parts].reshape(-1, width)
+        for first in range(0, out_ref.shape[0], tile):
+            place = pl.ds(first, tile)
+            total = lax.dot_general(
+                gated_ref[part, :, place], columns, (((0,), (0,)), ((), ())), preferred_element_type=F32
+            )
+            if part > 0:
+                total += total_ref[place]
+            if part < parts - 1:
+                total_ref[place] = total
+            else:
+                out_ref[place] = (total * scale).astype(BF16)
+
+
+def add_kernel(kept_ref, other_ref, out_ref):
+    out_ref[...] = (kept_ref[...] + other_ref[...].astype(F32)).astype(BF16)
 
 
 def shape(dims, kind):
@@ -319,10 +351,10 @@
         cost_estimate=cost(2),
         name="pack",
     )(value_input, filter_taps)
-    partner = after(partner, pair)
-    sides = jnp.stack([grad_output, partner])
-    grad_full = lax.all_gather(sides, "ch", axis=0, tiled=True, axis_index_groups=layers)
-    pair = exchange(pair, "seq")
+    near = lax.all_gather(grad_output, "ch", axis=0, tiled=False, axis_index_groups=layers)
+    far = [after(partner, pair)]
+    far += [lax.ppermute(far[0], "ch", ahead_by(ahead)) for ahead in (1, 2, 3)]
+    pair = exchange(after(pair, partner), "seq")
     packed, spec = pl.pallas_call(
         convolve_kernel,
         out_specs=(vmem, anywhere),
@@ -332,37 +364,28 @@
         cost_estimate=cost(3),
         name="convolve",
     )(pair, table)
-    conv, gated = pl.pallas_call(
-        gate_kernel,
-        out_shape=(shape((rows, channels), F32), shape((rows, channels), BF16)),
-        compiler_params=params(),
-        cost_estimate=cost(1),
-        name="gate",
-    )(exchange(packed, "seq"), gate_input)
-
-    gated_all = lax.all_gather(gated, "seq", axis=0, tiled=True)
-    split, quarter = width // 2, rows // ring
-    columns = pl.pallas_call(
-        columns_kernel,
-        in_specs=[smem, vmem],
-        out_shape=shape((shards, rows + quarter, split), BF16),
-        compiler_params=params(60),
-        cost_estimate=cost(2),
-        name="columns",
-    )(spot, grad_full)
-    columns = exchange(after(columns, gated), "seq")
-
     stream_scratch = [pltpu.VMEM((4, channels, channels), BF16), pltpu.SemaphoreType.DMA((4,))]
-    pre_grad, cotangent = pl.pallas_call(
+    direct = HALF + DIRECT * INNER
+    depth = direct + (4 - DIRECT) * HALF
+    pre_grad, send = pl.pallas_call(
         pre_grad_kernel,
-        in_specs=[smem, vmem, anywhere, vmem],
-        out_shape=(shape((rows, channels), F32), shape((shards, HALF, INNER), BF16)),
+        in_specs=[smem] + [vmem] * 5 + [anywhere, vmem],
+        out_shape=(shape((rows, channels), F32), shape((shards, depth, INNER), BF16)),
         scratch_shapes=stream_scratch,
         compiler_params=params(50),
         cost_estimate=cost(9),
         name="pre_grad",
-    )(spot, grad_full, out_weight, gate_input)
-    gate_grad = (pre_grad * conv).astype(BF16)
+    )(spot, near, *far, out_weight, gate_input)
+    gated, gate_grad = pl.pallas_call(
+        gate_kernel,
+        out_shape=[shape((rows, channels), BF16)] * 2,
+        compiler_params=params(),
+        cost_estimate=cost(1),
+        name="gate",
+    )(exchange(packed, "seq"), gate_input, pre_grad)
+
+    gated_all = lax.all_gather(gated, "seq", axis=0, tiled=True)
+    received = exchange(after(send, gated), "seq")
 
     order = (2, 1, 3, 0)
     parts = pl.pallas_call(
@@ -376,19 +399,19 @@
     )(spot, gated, out_weight)
     parts = [lax.ppermute(part, "ch", ahead_by(ahead)) if ahead else part for part, ahead in zip(parts, order)]
 
-    part = columns[:, rows:]
-    shared = [lax.ppermute(part, "ch", ahead_by(ahead)) for ahead in (1, 2, 3)]
-    parts = [after(got, (columns, cotangent)) for got in parts]
-    cotangent = exchange(after(cotangent, (columns, gate_grad)), "seq")
+    part = received[:, direct:]
+    shared = lax.ppermute(part, "ch", [(i, i ^ 2) for i in range(groups)])
     returned = pl.pallas_call(
         correlate_kernel,
+        grid=(1,),
         out_shape=shape((shards, rows, INNER), BF16),
-        in_specs=[vmem, anywhere, vmem],
+        in_specs=[pl.BlockSpec((shards, HALF, INNER), lambda step: (0, 0, 0)), anywhere, vmem],
+        out_specs=vmem,
         scratch_shapes=[spectra, pltpu.VMEM((shards, rows, INNER), BF16), planes, planes, pltpu.SemaphoreType.DMA],
         compiler_params=params(16),
         cost_estimate=cost(3),
         name="correlate",
-    )(after(cotangent, tuple(parts)), spec, table)
+    )(after(received, part), spec, table)
 
     parts = [after(got, returned) for got in parts]
     opposite = sum(part[1].astype(F32) for part in parts).astype(BF16)
@@ -399,15 +422,19 @@
 
     weight_grad = pl.pallas_call(
         functools.partial(weight_grad_kernel, scale),
-        grid=(4,),
-        in_specs=[smem, pl.BlockSpec((shards * rows, channels // 4), lambda step: (0, step))] + [anywhere] * ring,
-        out_specs=pl.BlockSpec((channels // 4, width), lambda step: (step, 0)),
+        in_specs=[smem, anywhere, anywhere, anywhere],
         out_shape=shape((channels, width), BF16),
-        scratch_shapes=[pltpu.VMEM((shards, rows, width), BF16), pltpu.SemaphoreType.DMA((ring + 1,))],
+        scratch_shapes=[
+            pltpu.VMEM((4, shards * rows // 4, channels), BF16),
+            pltpu.VMEM((shards, rows, width), BF16),
+            pltpu.VMEM((channels, width), F32),
+            pltpu.SemaphoreType.DMA((4,)),
+            pltpu.SemaphoreType.DMA((8 - DIRECT,)),
+        ],
         compiler_params=params(60),
         cost_estimate=cost(6),
         name="weight_grad",
-    )(spot, gated_all, columns, *shared)
+    )(spot, gated_all.reshape(4, shards * rows // 4, channels), received, shared)
     value_grad, filter_grad = pl.pallas_call(
         functools.partial(finish_kernel, scale),
         out_shape=(shape((rows, channels), BF16), shape((rows, channels), F32)),
@@ -415,8 +442,14 @@
         cost_estimate=cost(1),
         name="finish",
     )(after(returned, weight_grad))
-    opposite = after(opposite, weight_grad)
-    block_output = (kept + opposite.astype(F32)).astype(BF16)
+    opposite = after(opposite, (weight_grad, value_grad))
+    block_output = pl.pallas_call(
+        add_kernel,
+        out_shape=shape((rows, channels), BF16),
+        compiler_params=params(),
+        cost_estimate=cost(1),
+        name="add_opposite",
+    )(kept, opposite)
     return (block_output, gate_grad, value_grad, filter_grad, weight_grad)
 
 

time: 136 us -> 131 us (0.963)
  blocking collectives: 27.5 us -> 0 us
  waiting for transfers between devices: 14.3 us -> 33.1 us
  starting transfers between devices: 29.1 us -> 39.1 us
  other arithmetic: 6.5 us -> 1.77 us
    all_to_all x2 -> x0, blocking collectives: 27.5 us -> none  [exchange(): lax.all_to_all(array, axis, split_axis=0, concat_axis=0, tiled=True, axis...]
    all_to_all x3 -> x4, waiting for transfers between devices: 6.71 us -> 21.3 us  [exchange(): lax.all_to_all(array, axis, split_axis=0, concat_axis=0, tiled=True, axis...]
    ppermute x3 -> x4, waiting for transfers between devices: 0.01 us -> 7.33 us  [the longest x1 5.33 us: body(): shared = lax.ppermute(part, 'ch', [(i, i ^ 2) for i in range(groups)])]
    all_to_all x3 -> x4, starting transfers between devices: 15.4 us -> 22.1 us  [exchange(): lax.all_to_all(array, axis, split_axis=0, concat_axis=0, tiled=True, axis...]
    ppermute x3 -> x4, starting transfers between devices: 2.65 us -> 5.85 us  [the longest x3 4.46 us: body(): far += [lax.ppermute(far[0], 'ch', ahead_by(ahead)) for ahead in (1, 2, 3)]]
    convert_element_type x2 -> x0, other arithmetic: 2.79 us -> none  [the longest x1 2.03 us: body(): block_output = (kept + opposite.astype(F32)).astype(BF16)]
    ppermute x1, waiting for transfers between devices: 2.67 us -> 0.01 us  [body(): opposite = lax.ppermute(opposite, 'ch', across)]
    another operation x1 -> x0, other arithmetic: 1.79 us -> none  [body(): sides = jnp.stack([grad_output, partner])]
  transfers between devices with their start and end apart: 13 -> 15, of which waited for: 6 -> 6; matrix products, arithmetic and copies ran while one was open for 3% -> 2% of each run, Pallas kernels for 28% -> 27%
where the time goes in v3:
time: 131 us
  starting transfers between devices  39.1 us (30%)
  Pallas kernels  36.6 us (28%)
  waiting for transfers between devices  33.1 us (25%)
  between operations  14.2 us (11%)
  local copies, waits for them, and re-layouts  5.87 us (4%)
  other arithmetic  1.77 us (1%)
    all_to_all x4, starting transfers between devices, exchange(): lax.all_to_all(array, axis, split_axis=0, concat_axis=0, tiled=True, axis...  22.1 us
    all_to_all x4, waiting for transfers between devices, exchange(): lax.all_to_all(array, axis, split_axis=0, concat_axis=0, tiled=True, axis...  21.3 us
    pallas_call x1, Pallas kernels, body(): pl.pallas_call(pre_grad_kernel, in_specs=[smem] + [vmem] * 5 + [anywhere,...  9.32 us
    pallas_call x1, Pallas kernels, body(): pl.pallas_call(functools.partial(project_kernel, order), in_specs=[smem,...  8.45 us
    pallas_call x1, Pallas kernels, body(): pl.pallas_call(functools.partial(weight_grad_kernel, scale), in_specs=[sm...  6.25 us
    ppermute x1, waiting for transfers between devices, body(): shared = lax.ppermute(part, 'ch', [(i, i ^ 2) for i in range(groups)])  5.33 us
    unnamed x12, local copies, waits for them, and re-layouts  4.85 us
    ppermute x3, starting transfers between devices, body(): lax.ppermute(part, 'ch', ahead_by(ahead))  4.5 us
  transfers between devices with their start and end apart: 15, of which 6 were waited for; matrix products, arithmetic and copies ran while one was open for 2% of the time, Pallas kernels for 27%

profile of v3, /device:TPU:1, one launch (start us, length us, event | category | flops | bytes accessed | tf_op | source)
XLA Modules:
  0.0 130.7 jit_solution(2326048727252832842)
XLA Ops:
  7.2 0.0 all-gather.6.cloned.1.call-start
  7.2 0.7 all-gather.6.cloned.1.call-update
  7.9 3.8 %collective-permute-start = (bf16[128,1024]{1,0:T(8,128)(2,1)}, bf16[128,1024]{1,0:T(8,128)(2,1)S(1)}, u32[]{:S(2)}, u32[]{:S(2)}) collective-permute-start(bf16[128,1024]{1,0:T(8,128)(2,1)} %param.10), channel_id=1, source_target_pairs={{0,1},{1,0},{2,3},{3,2},{4,5},{5,4},{6,7},{7,6},{8,9},{9,8},{10,11... | collective-permute-start | bytes 786440 | tf_op jit(solution)/shard_map/ppermute | solution.py:346
  11.7 2.2 %pack.1 = bf16[16,128,128]{2,1,0:T(8,128)(2,1)} custom-call(bf16[128,1024]{1,0:T(8,128)(2,1)} %value_ref.1, f32[128,1024]{1,0:T(8,128)} %taps_ref.1), custom_call_target="tpu_custom_call" | custom-call | bytes 7000000 | tf_op jit(solution)/shard_map/pack/pallas_call | solution.py:347
  13.9 0.0 copy-start.3
  13.9 3.8 %collective-permute-done.far0_ref = bf16[128,1024]{1,0:T(8,128)(2,1)S(1)} collective-permute-done((bf16[128,1024]{1,0:T(8,128)(2,1)}, bf16[128,1024]{1,0:T(8,128)(2,1)S(1)}, u32[]{:S(2)}, u32[]{:S(2)}) %collective-permute-start) | collective-permute-done | bytes 262176 | tf_op jit(solution)/shard_map/ppermute | solution.py:346
  17.7 6.9 %all-to-all-start = ((bf16[16,128,128]{2,1,0:T(8,128)(2,1)}), bf16[16,128,128]{2,1,0:T(8,128)(2,1)S(1)}, u32[]{:S(2)}, u32[]{:S(2)}) async-start(bf16[16,128,128]{2,1,0:T(8,128)(2,1)} %pack.1), calls=%async_computation | async-start | bytes 1048576 | tf_op jit(solution)/shard_map/all_to_all | solution.py:320
  24.6 3.8 %collective-permute-start.3 = (bf16[128,1024]{1,0:T(8,128)(2,1)S(1)}, bf16[128,1024]{1,0:T(8,128)(2,1)S(1)}, u32[]{:S(2)}, u32[]{:S(2)}) collective-permute-start(bf16[128,1024]{1,0:T(8,128)(2,1)S(1)} %collective-permute-done.far0_ref), channel_id=1, source_target_pairs={{0,6},{1,7},{2,0},{3,1},{4,2},{5,3},{6,4},{7,5},{8,14},{9,15},{10,... | collective-permute-start | bytes 786440 | tf_op jit(solution)/shard_map/ppermute | solution.py:356
  28.3 0.0 collective-permute-start.2
  28.3 0.7 collective-permute-start.1
  29.0 5.4 %all-to-all-done.pair_ref = bf16[16,128,128]{2,1,0:T(8,128)(2,1)S(1)} async-done(((bf16[16,128,128]{2,1,0:T(8,128)(2,1)}), bf16[16,128,128]{2,1,0:T(8,128)(2,1)S(1)}, u32[]{:S(2)}, u32[]{:S(2)}) %all-to-all-start) | async-done | bytes 524320 | tf_op jit(solution)/shard_map/all_to_all | solution.py:320
  34.5 0.0 copy-start.1
  34.5 1.8 %copy-done.1 = bf16[42,256,128]{2,1,0:T(8,128)(2,1)S(1)} copy-done((bf16[42,256,128]{2,1,0:T(8,128)(2,1)S(1)}, bf16[42,256,128]{2,1,0:T(8,128)(2,1)}, u32[]{:S(2)}) %copy-start.1) | copy-done | bytes 2752536
  36.2 3.6 %convolve.1 = (bf16[16,64,128]{2,1,0:T(8,128)(2,1)}, bf16[17,256,128]{2,1,0:T(8,128)(2,1)S(1)}) custom-call(bf16[16,128,128]{2,1,0:T(8,128)(2,1)S(1)} %all-to-all-done.pair_ref, bf16[42,256,128]{2,1,0:T(8,128)(2,1)S(1)} %copy-done.1), custom_call_target="tpu_custom_call" | custom-call | bytes 10500000 | tf_op jit(solution)/shard_map/convolve/pallas_call | solution.py:358
  39.9 4.4 %all-to-all-start.1 = ((bf16[16,64,128]{2,1,0:T(8,128)(2,1)}), bf16[16,64,128]{2,1,0:T(8,128)(2,1)S(1)}, u32[]{:S(2)}, u32[]{:S(2)}) async-start(bf16[16,64,128]{2,1,0:T(8,128)(2,1)} %get-tuple-element.28), calls=%async_computation.1 | async-start | bytes 524288 | tf_op jit(solution)/shard_map/all_to_all | solution.py:320
  44.3 0.0 all-gather.4.cloned.1.call-start
  44.4 0.1 pad_add_fusion.spot_ref
  44.4 0.0 copy-start.5
  44.4 0.5 collective-permute-done.3.far3_ref
  44.9 0.0 collective-permute-done.2.far2_ref
  44.9 1.5 %collective-permute-done.1.far1_ref = bf16[128,1024]{1,0:T(8,128)(2,1)S(1)} collective-permute-done((bf16[128,1024]{1,0:T(8,128)(2,1)S(1)}, bf16[128,1024]{1,0:T(8,128)(2,1)S(1)}, u32[]{:S(2)}, u32[]{:S(2)}) %collective-permute-start.1) | collective-permute-done | bytes 262176 | tf_op jit(solution)/shard_map/ppermute | solution.py:356
  46.4 0.0 all-gather.6.cloned.1.call-done
  46.4 0.0 copy-done.3
  46.4 0.0 copy-start.4
  46.4 1.2 copy-done.4
  47.7 9.3 %pre_grad.1 = (f32[128,1024]{1,0:T(8,128)S(1)}, bf16[16,384,128]{2,1,0:T(8,128)(2,1)}) custom-call(s32[2]{0:T(128)S(1)} %pad_add_fusion.spot_ref, bf16[4,128,1024]{2,1,0:T(8,128)(2,1)S(1)} %bitcast.8, bf16[128,1024]{1,0:T(8,128)(2,1)S(1)} %collective-permute-done.far0_ref, bf16[128,1024]{1,0:T(8,128)(2,1)S(1)} %collective-permute-done.1.far1_ref, ...), custom_call_target="tpu_custom_call" | custom-call | bytes 31500000 | tf_op jit(solution)/shard_map/pre_grad/pallas_call | solution.py:370
  57.0 0.0 all-to-all-done.1.recv_ref
  57.0 1.0 gate.1
  58.0 0.0 all-gather.4.cloned.1.call-update
  58.0 5.8 %all-to-all-start.2 = ((bf16[16,384,128]{2,1,0:T(8,128)(2,1)}), bf16[16,384,128]{2,1,0:T(8,128)(2,1)S(1)}, u32[]{:S(2)}, u32[]{:S(2)}) async-start(bf16[16,384,128]{2,1,0:T(8,128)(2,1)} %get-tuple-element.34), calls=%async_computation.2 | async-start | bytes 3145728 | tf_op jit(solution)/shard_map/all_to_all | solution.py:320
  63.8 0.0 copy-done.5
  63.8 8.4 %project.1 = (bf16[2,128,1024]{2,1,0:T(8,128)(2,1)}, bf16[2,128,1024]{2,1,0:T(8,128)(2,1)}, bf16[2,128,1024]{2,1,0:T(8,128)(2,1)}, bf16[2,128,1024]{2,1,0:T(8,128)(2,1)S(1)}) custom-call(s32[2]{0:T(128)S(1)} %pad_add_fusion.spot_ref, bf16[128,1024]{1,0:T(8,128)(2,1)} %get-tuple-element.31.gated_ref, bf16[1024,8192]{1,0:T(8,128)(2,1)} %weight_hbm.3), custom_call_target="tpu_custom_call" | custom-call | bytes 28000000 | tf_op jit(solution)/shard_map/project/pallas_call | solution.py:391
  72.3 1.8 %collective-permute-start.4 = (bf16[2,128,1024]{2,1,0:T(8,128)(2,1)}, bf16[2,128,1024]{2,1,0:T(8,128)(2,1)}, u32[]{:S(2)}, u32[]{:S(2)}) collective-permute-start(bf16[2,128,1024]{2,1,0:T(8,128)(2,1)} %get-tuple-element.32), channel_id=1, source_target_pairs={{0,4},{1,5},{2,6},{3,7},{4,0},{5,1},{6,2},{7,3},{8,12},{9,13},{10,... | collective-permute-start | bytes 1572872 | tf_op jit(solution)/shard_map/ppermute | solution.py:400
  74.1 1.2 collective-permute-start.5
  75.3 1.5 %collective-permute-start.6 = (bf16[2,128,1024]{2,1,0:T(8,128)(2,1)}, bf16[2,128,1024]{2,1,0:T(8,128)(2,1)}, u32[]{:S(2)}, u32[]{:S(2)}) collective-permute-start(bf16[2,128,1024]{2,1,0:T(8,128)(2,1)} %get-tuple-element.40), channel_id=1, source_target_pairs={{0,6},{1,7},{2,0},{3,1},{4,2},{5,3},{6,4},{7,5},{8,14},{9,15},{10,... | collective-permute-start | bytes 1572872 | tf_op jit(solution)/shard_map/ppermute | solution.py:400
  76.8 15.9 %all-to-all-done.2.grad_ref.received_hbm = bf16[16,384,128]{2,1,0:T(8,128)(2,1)S(1)} async-done(((bf16[16,384,128]{2,1,0:T(8,128)(2,1)}), bf16[16,384,128]{2,1,0:T(8,128)(2,1)S(1)}, u32[]{:S(2)}, u32[]{:S(2)}) %all-to-all-start.2) | async-done | bytes 1572896 | tf_op jit(solution)/shard_map/all_to_all | solution.py:320
  92.7 0.0 copy-start
  92.7 1.0 slice.36
  93.7 1.4 %collective-permute-start.8 = (bf16[16,192,128]{2,1,0:T(8,128)(2,1)}, bf16[16,192,128]{2,1,0:T(8,128)(2,1)}, u32[]{:S(2)}, u32[]{:S(2)}) collective-permute-start(bf16[16,192,128]{2,1,0:T(8,128)(2,1)} %slice.36), channel_id=1, source_target_pairs={{0,2},{1,3},{2,0},{3,1},{4,6},{5,7},{6,4},{7,5},{8,10},{9,11},{10,... | collective-permute-start | bytes 2359304 | tf_op jit(solution)/shard_map/ppermute | solution.py:403
  95.1 0.0 copy-start.2
  95.1 1.8 %copy-done.2 = bf16[42,256,128]{2,1,0:T(8,128)(2,1)S(1)} copy-done((bf16[42,256,128]{2,1,0:T(8,128)(2,1)S(1)}, bf16[42,256,128]{2,1,0:T(8,128)(2,1)}, u32[]{:S(2)}) %copy-start.2) | copy-done | bytes 2752536
  96.9 3.9 %correlate.1 = bf16[16,128,128]{2,1,0:T(8,128)(2,1)} custom-call(bf16[16,384,128]{2,1,0:T(8,128)(2,1)S(1)} %all-to-all-done.2.grad_ref.received_hbm, bf16[17,256,128]{2,1,0:T(8,128)(2,1)S(1)} %get-tuple-element.36.spec_hbm, bf16[42,256,128]{2,1,0:T(8,128)(2,1)S(1)} %copy-done.2), custom_call_target="tpu_custom_call" | custom-call | bytes 10500000 | tf_op jit(solution)/shard_map/correlate/pallas_call | solution.py:404
  100.8 0.0 copy-done
  100.8 5.1 %all-to-all-start.3 = ((bf16[16,128,128]{2,1,0:T(8,128)(2,1)}), bf16[16,128,128]{2,1,0:T(8,128)(2,1)S(1)}, u32[]{:S(2)}, u32[]{:S(2)}) async-start(bf16[16,128,128]{2,1,0:T(8,128)(2,1)} %correlate.1), calls=%async_computation.3 | async-start | bytes 1048576 | tf_op jit(solution)/shard_map/all_to_all | solution.py:320
  105.9 0.0 collective-permute-done.4
  105.9 0.0 collective-permute-done.5
  105.9 0.0 collective-permute-done.6
  105.9 1.7 %fusion = (bf16[128,1024]{1,0:T(8,128)(2,1)S(1)}, f32[128,1024]{1,0:T(8,128)S(1)}) fusion(bf16[2,128,1024]{2,1,0:T(8,128)(2,1)S(1)} %get-tuple-element.43, bf16[2,128,1024]{2,1,0:T(8,128)(2,1)} %collective-permute-done.6, bf16[2,128,1024]{2,1,0:T(8,128)(2,1)} %collective-permute-done.5, bf16[2,128,1024]{2,1,0:T(8,128)(2,1)} %collective-permute-done.4), kind=kLoop, calls=%fused_computation.2 | loop fusion | flops 1966080 | bytes 2883584 | tf_op jit(solution)/shard_map/add | solution.py:417
  107.6 2.7 %collective-permute-start.7 = (bf16[128,1024]{1,0:T(8,128)(2,1)S(1)}, bf16[128,1024]{1,0:T(8,128)(2,1)S(1)}, u32[]{:S(2)}, u32[]{:S(2)}) collective-permute-start(bf16[128,1024]{1,0:T(8,128)(2,1)S(1)} %get-tuple-element.49), channel_id=1, source_target_pairs={{0,1},{1,0},{2,3},{3,2},{4,5},{5,4},{6,7},{7,6},{8,9},{9,8},{10,11... | collective-permute-start | bytes 786440 | tf_op jit(solution)/shard_map/ppermute | solution.py:421
  110.3 5.3 %collective-permute-done.8.shared_hbm = bf16[16,192,128]{2,1,0:T(8,128)(2,1)} collective-permute-done((bf16[16,192,128]{2,1,0:T(8,128)(2,1)}, bf16[16,192,128]{2,1,0:T(8,128)(2,1)}, u32[]{:S(2)}, u32[]{:S(2)}) %collective-permute-start.8) | collective-permute-done | bytes 786464 | tf_op jit(solution)/shard_map/ppermute | solution.py:403
  115.7 0.0 all-gather.4.cloned.1.call-done
  115.7 6.3 %weight_grad.1 = bf16[1024,512]{1,0:T(8,128)(2,1)} custom-call(s32[2]{0:T(128)} %copy-done.5, bf16[4,512,1024]{2,1,0:T(8,128)(2,1)} %bitcast.9, bf16[16,384,128]{2,1,0:T(8,128)(2,1)} %copy-done, bf16[16,192,128]{2,1,0:T(8,128)(2,1)} %collective-permute-done.8.shared_hbm), custom_call_target="tpu_custom_call" | custom-call | bytes 21000000 | tf_op jit(solution)/shard_map/weight_grad/pallas_call | solution.py:423
  121.9 0.0 all-to-all-done.3.recv_ref
  122.0 1.1 finish.1
  123.1 0.0 collective-permute-done.7.other_ref
  123.1 0.7 add_opposite.1
Async XLA Ops:
  7.2 39.3 %all-gather.6.cloned.1.call-start = ((), (), s32[]{:S(2)}) async-start(), calls=%async_computation.5 | async-start | bytes 1310720 | tf_op jit(solution)/shard_map/all_gather | solution.py:354
  7.9 9.8 %collective-permute-start = (bf16[128,1024]{1,0:T(8,128)(2,1)}, bf16[128,1024]{1,0:T(8,128)(2,1)S(1)}, u32[]{:S(2)}, u32[]{:S(2)}) collective-permute-start(bf16[128,1024]{1,0:T(8,128)(2,1)} %param.10), channel_id=1, source_target_pairs={{0,1},{1,0},{2,3},{3,2},{4,5},{5,4},{6,7},{7,6},{8,9},{9,8},{10,11... | collective-permute-start | bytes 786440 | tf_op jit(solution)/shard_map/ppermute | solution.py:346
  13.9 32.5 %copy-start.3 = (bf16[128,1024]{1,0:T(8,128)(2,1)S(1)}, bf16[128,1024]{1,0:T(8,128)(2,1)}, u32[]{:S(2)}) copy-start(bf16[128,1024]{1,0:T(8,128)(2,1)} %gate_ref.3) | copy-start | bytes 786436
  17.7 16.8 %all-to-all-start = ((bf16[16,128,128]{2,1,0:T(8,128)(2,1)}), bf16[16,128,128]{2,1,0:T(8,128)(2,1)S(1)}, u32[]{:S(2)}, u32[]{:S(2)}) async-start(bf16[16,128,128]{2,1,0:T(8,128)(2,1)} %pack.1), calls=%async_computation | async-start | bytes 1048576 | tf_op jit(solution)/shard_map/all_to_all | solution.py:320
  24.6 20.4 %collective-permute-start.3 = (bf16[128,1024]{1,0:T(8,128)(2,1)S(1)}, bf16[128,1024]{1,0:T(8,128)(2,1)S(1)}, u32[]{:S(2)}, u32[]{:S(2)}) collective-permute-start(bf16[128,1024]{1,0:T(8,128)(2,1)S(1)} %collective-permute-done.far0_ref), channel_id=1, source_target_pairs={{0,6},{1,7},{2,0},{3,1},{4,2},{5,3},{6,4},{7,5},{8,14},{9,15},{10,... | collective-permute-start | bytes 786440 | tf_op jit(solution)/shard_map/ppermute | solution.py:356
  28.3 16.6 %collective-permute-start.2 = (bf16[128,1024]{1,0:T(8,128)(2,1)S(1)}, bf16[128,1024]{1,0:T(8,128)(2,1)S(1)}, u32[]{:S(2)}, u32[]{:S(2)}) collective-permute-start(bf16[128,1024]{1,0:T(8,128)(2,1)S(1)} %collective-permute-done.far0_ref), channel_id=1, source_target_pairs={{0,4},{1,5},{2,6},{3,7},{4,0},{5,1},{6,2},{7,3},{8,12},{9,13},{10,... | collective-permute-start | bytes 786440 | tf_op jit(solution)/shard_map/ppermute | solution.py:356
  28.3 18.1 %collective-permute-start.1 = (bf16[128,1024]{1,0:T(8,128)(2,1)S(1)}, bf16[128,1024]{1,0:T(8,128)(2,1)S(1)}, u32[]{:S(2)}, u32[]{:S(2)}) collective-permute-start(bf16[128,1024]{1,0:T(8,128)(2,1)S(1)} %collective-permute-done.far0_ref), channel_id=1, source_target_pairs={{0,2},{1,3},{2,4},{3,5},{4,6},{5,7},{6,0},{7,1},{8,10},{9,11},{10,... | collective-permute-start | bytes 786440 | tf_op jit(solution)/shard_map/ppermute | solution.py:356
  34.5 1.8 %copy-start.1 = (bf16[42,256,128]{2,1,0:T(8,128)(2,1)S(1)}, bf16[42,256,128]{2,1,0:T(8,128)(2,1)}, u32[]{:S(2)}) copy-start(bf16[42,256,128]{2,1,0:T(8,128)(2,1)} %constant.30.clone.table_ref) | copy-start | bytes 8257540
  39.9 17.1 %all-to-all-start.1 = ((bf16[16,64,128]{2,1,0:T(8,128)(2,1)}), bf16[16,64,128]{2,1,0:T(8,128)(2,1)S(1)}, u32[]{:S(2)}, u32[]{:S(2)}) async-start(bf16[16,64,128]{2,1,0:T(8,128)(2,1)} %get-tuple-element.28), calls=%async_computation.1 | async-start | bytes 524288 | tf_op jit(solution)/shard_map/all_to_all | solution.py:320
  44.3 71.4 %all-gather.4.cloned.1.call-start = ((), (), s32[]{:S(2)}) async-start(), calls=%async_computation.4 | async-start | bytes 4456448 | tf_op jit(solution)/shard_map/all_gather | solution.py:387
  44.4 19.4 %copy-start.5 = (s32[2]{0:T(128)}, s32[2]{0:T(128)S(1)}, u32[]{:S(2)}) copy-start(s32[2]{0:T(128)S(1)} %pad_add_fusion.spot_ref) | copy-start | bytes 28
  46.4 1.2 copy-start.4
  58.0 34.6 %all-to-all-start.2 = ((bf16[16,384,128]{2,1,0:T(8,128)(2,1)}), bf16[16,384,128]{2,1,0:T(8,128)(2,1)S(1)}, u32[]{:S(2)}, u32[]{:S(2)}) async-start(bf16[16,384,128]{2,1,0:T(8,128)(2,1)} %get-tuple-element.34), calls=%async_computation.2 | async-start | bytes 3145728 | tf_op jit(solution)/shard_map/all_to_all | solution.py:320
  72.3 33.6 %collective-permute-start.4 = (bf16[2,128,1024]{2,1,0:T(8,128)(2,1)}, bf16[2,128,1024]{2,1,0:T(8,128)(2,1)}, u32[]{:S(2)}, u32[]{:S(2)}) collective-permute-start(bf16[2,128,1024]{2,1,0:T(8,128)(2,1)} %get-tuple-element.32), channel_id=1, source_target_pairs={{0,4},{1,5},{2,6},{3,7},{4,0},{5,1},{6,2},{7,3},{8,12},{9,13},{10,... | collective-permute-start | bytes 1572872 | tf_op jit(solution)/shard_map/ppermute | solution.py:400
  74.1 31.8 %collective-permute-start.5 = (bf16[2,128,1024]{2,1,0:T(8,128)(2,1)}, bf16[2,128,1024]{2,1,0:T(8,128)(2,1)}, u32[]{:S(2)}, u32[]{:S(2)}) collective-permute-start(bf16[2,128,1024]{2,1,0:T(8,128)(2,1)} %get-tuple-element.38), channel_id=1, source_target_pairs={{0,2},{1,3},{2,4},{3,5},{4,6},{5,7},{6,0},{7,1},{8,10},{9,11},{10,... | collective-permute-start | bytes 1572872 | tf_op jit(solution)/shard_map/ppermute | solution.py:400
  75.3 30.6 %collective-permute-start.6 = (bf16[2,128,1024]{2,1,0:T(8,128)(2,1)}, bf16[2,128,1024]{2,1,0:T(8,128)(2,1)}, u32[]{:S(2)}, u32[]{:S(2)}) collective-permute-start(bf16[2,128,1024]{2,1,0:T(8,128)(2,1)} %get-tuple-element.40), channel_id=1, source_target_pairs={{0,6},{1,7},{2,0},{3,1},{4,2},{5,3},{6,4},{7,5},{8,14},{9,15},{10,... | collective-permute-start | bytes 1572872 | tf_op jit(solution)/shard_map/ppermute | solution.py:400
  92.7 8.1 %copy-start = (bf16[16,384,128]{2,1,0:T(8,128)(2,1)}, bf16[16,384,128]{2,1,0:T(8,128)(2,1)S(1)}, u32[]{:S(2)}) copy-start(bf16[16,384,128]{2,1,0:T(8,128)(2,1)S(1)} %all-to-all-done.2.grad_ref.received_hbm) | copy-start | bytes 4718596
  93.7 22.0 %collective-permute-start.8 = (bf16[16,192,128]{2,1,0:T(8,128)(2,1)}, bf16[16,192,128]{2,1,0:T(8,128)(2,1)}, u32[]{:S(2)}, u32[]{:S(2)}) collective-permute-start(bf16[16,192,128]{2,1,0:T(8,128)(2,1)} %slice.36), channel_id=1, source_target_pairs={{0,2},{1,3},{2,0},{3,1},{4,6},{5,7},{6,4},{7,5},{8,10},{9,11},{10,... | collective-permute-start | bytes 2359304 | tf_op jit(solution)/shard_map/ppermute | solution.py:403
  95.1 1.8 %copy-start.2 = (bf16[42,256,128]{2,1,0:T(8,128)(2,1)S(1)}, bf16[42,256,128]{2,1,0:T(8,128)(2,1)}, u32[]{:S(2)}) copy-start(bf16[42,256,128]{2,1,0:T(8,128)(2,1)} %constant.30.clone.table_ref) | copy-start | bytes 8257540
  100.8 21.1 %all-to-all-start.3 = ((bf16[16,128,128]{2,1,0:T(8,128)(2,1)}), bf16[16,128,128]{2,1,0:T(8,128)(2,1)S(1)}, u32[]{:S(2)}, u32[]{:S(2)}) async-start(bf16[16,128,128]{2,1,0:T(8,128)(2,1)} %correlate.1), calls=%async_computation.3 | async-start | bytes 1048576 | tf_op jit(solution)/shard_map/all_to_all | solution.py:320
  107.6 15.5 %collective-permute-start.7 = (bf16[128,1024]{1,0:T(8,128)(2,1)S(1)}, bf16[128,1024]{1,0:T(8,128)(2,1)S(1)}, u32[]{:S(2)}, u32[]{:S(2)}) collective-permute-start(bf16[128,1024]{1,0:T(8,128)(2,1)S(1)} %get-tuple-element.49), channel_id=1, source_target_pairs={{0,1},{1,0},{2,3},{3,2},{4,5},{5,4},{6,7},{7,6},{8,9},{9,8},{10,11... | collective-permute-start | bytes 786440 | tf_op jit(solution)/shard_map/ppermute | solution.py:421
Sparse Core Ops, SparseCore 0:
  9.7 34.1 all-gather.5
  58.2 50.3 all-gather.3

commit v4 on v3

--- a/solution.py
+++ b/solution.py
@@ -385,7 +385,7 @@
     )(exchange(packed, "seq"), gate_input, pre_grad)
 
     gated_all = lax.all_gather(gated, "seq", axis=0, tiled=True)
-    received = exchange(after(send, gated), "seq")
+    received = exchange(send, "seq")
 
     order = (2, 1, 3, 0)
     parts = pl.pallas_call(

time: 131 us -> 130 us (level)
  transfers between devices with their start and end apart: 15 -> 15, of which waited for: 6 -> 5; matrix products, arithmetic and copies ran while one was open for 2% -> 2% of each run, Pallas kernels for 27% -> 27%
where the time goes in v4:
time: 130 us
  starting transfers between devices  39.1 us (30%)
  Pallas kernels  36.6 us (28%)
  waiting for transfers between devices  32.1 us (25%)
  between operations  14.2 us (11%)
  local copies, waits for them, and re-layouts  5.83 us (4%)
  other arithmetic  1.78 us (1%)
    all_to_all x4, starting transfers between devices, exchange(): lax.all_to_all(array, axis, split_axis=0, concat_axis=0, tiled=True, axis...  22.8 us
    all_to_all x4, waiting for transfers between devices, exchange(): lax.all_to_all(array, axis, split_axis=0, concat_axis=0, tiled=True, axis...  20.9 us
    pallas_call x1, Pallas kernels, body(): pl.pallas_call(pre_grad_kernel, in_specs=[smem] + [vmem] * 5 + [anywhere,...  9.32 us
    pallas_call x1, Pallas kernels, body(): pl.pallas_call(functools.partial(project_kernel, order), in_specs=[smem,...  8.48 us
    pallas_call x1, Pallas kernels, body(): pl.pallas_call(functools.partial(weight_grad_kernel, scale), in_specs=[sm...  6.26 us
    ppermute x3, starting transfers between devices, body(): far += [lax.ppermute(far[0], 'ch', ahead_by(ahead)) for ahead in (1, 2, 3)]  5.67 us
    unnamed x12, local copies, waits for them, and re-layouts  4.81 us
    ppermute x1, waiting for transfers between devices, body(): shared = lax.ppermute(part, 'ch', [(i, i ^ 2) for i in range(groups)])  4.73 us
  transfers between devices with their start and end apart: 15, of which 5 were waited for; matrix products, arithmetic and copies ran while one was open for 2% of the time, Pallas kernels for 27%

profile of v4, /device:TPU:1, one launch (start us, length us, event | category | flops | bytes accessed | tf_op | source)
XLA Modules:
  0.0 129.6 jit_solution(2288585480383043130)
XLA Ops:
  7.2 0.0 all-gather.6.cloned.1.call-start
  7.2 0.7 all-gather.6.cloned.1.call-update
  7.9 3.8 %collective-permute-start = (bf16[128,1024]{1,0:T(8,128)(2,1)}, bf16[128,1024]{1,0:T(8,128)(2,1)S(1)}, u32[]{:S(2)}, u32[]{:S(2)}) collective-permute-start(bf16[128,1024]{1,0:T(8,128)(2,1)} %param.10), channel_id=1, source_target_pairs={{0,1},{1,0},{2,3},{3,2},{4,5},{5,4},{6,7},{7,6},{8,9},{9,8},{10,11... | collective-permute-start | bytes 786440 | tf_op jit(solution)/shard_map/ppermute | solution.py:346
  11.7 2.2 %pack.1 = bf16[16,128,128]{2,1,0:T(8,128)(2,1)} custom-call(bf16[128,1024]{1,0:T(8,128)(2,1)} %value_ref.1, f32[128,1024]{1,0:T(8,128)} %taps_ref.1), custom_call_target="tpu_custom_call" | custom-call | bytes 7000000 | tf_op jit(solution)/shard_map/pack/pallas_call | solution.py:347
  13.9 0.0 copy-start.3
  13.9 3.8 %collective-permute-done.far0_ref = bf16[128,1024]{1,0:T(8,128)(2,1)S(1)} collective-permute-done((bf16[128,1024]{1,0:T(8,128)(2,1)}, bf16[128,1024]{1,0:T(8,128)(2,1)S(1)}, u32[]{:S(2)}, u32[]{:S(2)}) %collective-permute-start) | collective-permute-done | bytes 262176 | tf_op jit(solution)/shard_map/ppermute | solution.py:346
  17.7 6.9 %all-to-all-start = ((bf16[16,128,128]{2,1,0:T(8,128)(2,1)}), bf16[16,128,128]{2,1,0:T(8,128)(2,1)S(1)}, u32[]{:S(2)}, u32[]{:S(2)}) async-start(bf16[16,128,128]{2,1,0:T(8,128)(2,1)} %pack.1), calls=%async_computation | async-start | bytes 1048576 | tf_op jit(solution)/shard_map/all_to_all | solution.py:320
  24.6 1.6 %collective-permute-start.1 = (bf16[128,1024]{1,0:T(8,128)(2,1)S(1)}, bf16[128,1024]{1,0:T(8,128)(2,1)S(1)}, u32[]{:S(2)}, u32[]{:S(2)}) collective-permute-start(bf16[128,1024]{1,0:T(8,128)(2,1)S(1)} %collective-permute-done.far0_ref), channel_id=1, source_target_pairs={{0,2},{1,3},{2,4},{3,5},{4,6},{5,7},{6,0},{7,1},{8,10},{9,11},{10,... | collective-permute-start | bytes 786440 | tf_op jit(solution)/shard_map/ppermute | solution.py:356
  26.2 3.3 %collective-permute-start.2 = (bf16[128,1024]{1,0:T(8,128)(2,1)S(1)}, bf16[128,1024]{1,0:T(8,128)(2,1)S(1)}, u32[]{:S(2)}, u32[]{:S(2)}) collective-permute-start(bf16[128,1024]{1,0:T(8,128)(2,1)S(1)} %collective-permute-done.far0_ref), channel_id=1, source_target_pairs={{0,4},{1,5},{2,6},{3,7},{4,0},{5,1},{6,2},{7,3},{8,12},{9,13},{10,... | collective-permute-start | bytes 786440 | tf_op jit(solution)/shard_map/ppermute | solution.py:356
  29.5 0.7 collective-permute-start.3
  30.2 4.2 %all-to-all-done.pair_ref = bf16[16,128,128]{2,1,0:T(8,128)(2,1)S(1)} async-done(((bf16[16,128,128]{2,1,0:T(8,128)(2,1)}), bf16[16,128,128]{2,1,0:T(8,128)(2,1)S(1)}, u32[]{:S(2)}, u32[]{:S(2)}) %all-to-all-start) | async-done | bytes 524320 | tf_op jit(solution)/shard_map/all_to_all | solution.py:320
  34.5 0.0 copy-start.1
  34.5 1.8 %copy-done.1 = bf16[42,256,128]{2,1,0:T(8,128)(2,1)S(1)} copy-done((bf16[42,256,128]{2,1,0:T(8,128)(2,1)S(1)}, bf16[42,256,128]{2,1,0:T(8,128)(2,1)}, u32[]{:S(2)}) %copy-start.1) | copy-done | bytes 2752536
  36.3 3.6 %convolve.1 = (bf16[16,64,128]{2,1,0:T(8,128)(2,1)}, bf16[17,256,128]{2,1,0:T(8,128)(2,1)S(1)}) custom-call(bf16[16,128,128]{2,1,0:T(8,128)(2,1)S(1)} %all-to-all-done.pair_ref, bf16[42,256,128]{2,1,0:T(8,128)(2,1)S(1)} %copy-done.1), custom_call_target="tpu_custom_call" | custom-call | bytes 10500000 | tf_op jit(solution)/shard_map/convolve/pallas_call | solution.py:358
  39.9 4.4 %all-to-all-start.1 = ((bf16[16,64,128]{2,1,0:T(8,128)(2,1)}), bf16[16,64,128]{2,1,0:T(8,128)(2,1)S(1)}, u32[]{:S(2)}, u32[]{:S(2)}) async-start(bf16[16,64,128]{2,1,0:T(8,128)(2,1)} %get-tuple-element.27), calls=%async_computation.1 | async-start | bytes 524288 | tf_op jit(solution)/shard_map/all_to_all | solution.py:320
  44.3 0.0 all-gather.4.cloned.1.call-start
  44.4 0.1 pad_add_fusion.spot_ref
  44.4 0.0 copy-start.5
  44.4 0.0 collective-permute-done.1.far1_ref
  44.4 2.0 %collective-permute-done.2.far2_ref = bf16[128,1024]{1,0:T(8,128)(2,1)S(1)} collective-permute-done((bf16[128,1024]{1,0:T(8,128)(2,1)S(1)}, bf16[128,1024]{1,0:T(8,128)(2,1)S(1)}, u32[]{:S(2)}, u32[]{:S(2)}) %collective-permute-start.2) | collective-permute-done | bytes 262176 | tf_op jit(solution)/shard_map/ppermute | solution.py:356
  46.4 0.0 collective-permute-done.3.far3_ref
  46.4 0.0 all-gather.6.cloned.1.call-done
  46.4 0.0 copy-done.3
  46.4 0.0 copy-start.4
  46.4 1.2 copy-done.4
  47.6 9.3 %pre_grad.1 = (f32[128,1024]{1,0:T(8,128)S(1)}, bf16[16,384,128]{2,1,0:T(8,128)(2,1)}) custom-call(s32[2]{0:T(128)S(1)} %pad_add_fusion.spot_ref, bf16[4,128,1024]{2,1,0:T(8,128)(2,1)S(1)} %bitcast.8, bf16[128,1024]{1,0:T(8,128)(2,1)S(1)} %collective-permute-done.far0_ref, bf16[128,1024]{1,0:T(8,128)(2,1)S(1)} %collective-permute-done.1.far1_ref, ...), custom_call_target="tpu_custom_call" | custom-call | bytes 31500000 | tf_op jit(solution)/shard_map/pre_grad/pallas_call | solution.py:370
  57.0 0.0 all-to-all-done.1.recv_ref
  57.0 1.0 gate.1
  58.0 0.0 all-gather.4.cloned.1.call-update
  58.0 5.9 %all-to-all-start.2 = ((bf16[16,384,128]{2,1,0:T(8,128)(2,1)}), bf16[16,384,128]{2,1,0:T(8,128)(2,1)S(1)}, u32[]{:S(2)}, u32[]{:S(2)}) async-start(bf16[16,384,128]{2,1,0:T(8,128)(2,1)} %get-tuple-element.32), calls=%async_computation.2 | async-start | bytes 3145728 | tf_op jit(solution)/shard_map/all_to_all | solution.py:320
  64.0 0.0 copy-done.5
  64.0 8.5 %project.1 = (bf16[2,128,1024]{2,1,0:T(8,128)(2,1)}, bf16[2,128,1024]{2,1,0:T(8,128)(2,1)}, bf16[2,128,1024]{2,1,0:T(8,128)(2,1)}, bf16[2,128,1024]{2,1,0:T(8,128)(2,1)S(1)}) custom-call(s32[2]{0:T(128)S(1)} %pad_add_fusion.spot_ref, bf16[128,1024]{1,0:T(8,128)(2,1)} %get-tuple-element.30.gated_ref, bf16[1024,8192]{1,0:T(8,128)(2,1)} %weight_hbm.3), custom_call_target="tpu_custom_call" | custom-call | bytes 28000000 | tf_op jit(solution)/shard_map/project/pallas_call | solution.py:391
  72.5 2.3 %collective-permute-start.6 = (bf16[2,128,1024]{2,1,0:T(8,128)(2,1)}, bf16[2,128,1024]{2,1,0:T(8,128)(2,1)}, u32[]{:S(2)}, u32[]{:S(2)}) collective-permute-start(bf16[2,128,1024]{2,1,0:T(8,128)(2,1)} %get-tuple-element.38), channel_id=1, source_target_pairs={{0,6},{1,7},{2,0},{3,1},{4,2},{5,3},{6,4},{7,5},{8,14},{9,15},{10,... | collective-permute-start | bytes 1572872 | tf_op jit(solution)/shard_map/ppermute | solution.py:400
  74.7 0.0 collective-permute-start.5
  74.7 1.2 collective-permute-start.4
  76.0 16.7 %all-to-all-done.2.grad_ref.received_hbm = bf16[16,384,128]{2,1,0:T(8,128)(2,1)S(1)} async-done(((bf16[16,384,128]{2,1,0:T(8,128)(2,1)}), bf16[16,384,128]{2,1,0:T(8,128)(2,1)S(1)}, u32[]{:S(2)}, u32[]{:S(2)}) %all-to-all-start.2) | async-done | bytes 1572896 | tf_op jit(solution)/shard_map/all_to_all | solution.py:320
  92.6 0.0 copy-start
  92.6 1.0 slice.36
  93.7 0.7 collective-permute-start.8
  94.3 0.0 copy-start.2
  94.3 1.8 %copy-done.2 = bf16[42,256,128]{2,1,0:T(8,128)(2,1)S(1)} copy-done((bf16[42,256,128]{2,1,0:T(8,128)(2,1)S(1)}, bf16[42,256,128]{2,1,0:T(8,128)(2,1)}, u32[]{:S(2)}) %copy-start.2) | copy-done | bytes 2752536
  96.1 3.9 %correlate.1 = bf16[16,128,128]{2,1,0:T(8,128)(2,1)} custom-call(bf16[16,384,128]{2,1,0:T(8,128)(2,1)S(1)} %all-to-all-done.2.grad_ref.received_hbm, bf16[17,256,128]{2,1,0:T(8,128)(2,1)S(1)} %get-tuple-element.34.spec_hbm, bf16[42,256,128]{2,1,0:T(8,128)(2,1)S(1)} %copy-done.2), custom_call_target="tpu_custom_call" | custom-call | bytes 10500000 | tf_op jit(solution)/shard_map/correlate/pallas_call | solution.py:404
  100.0 0.0 copy-done
  100.0 5.5 %all-to-all-start.3 = ((bf16[16,128,128]{2,1,0:T(8,128)(2,1)}), bf16[16,128,128]{2,1,0:T(8,128)(2,1)S(1)}, u32[]{:S(2)}, u32[]{:S(2)}) async-start(bf16[16,128,128]{2,1,0:T(8,128)(2,1)} %correlate.1), calls=%async_computation.3 | async-start | bytes 1048576 | tf_op jit(solution)/shard_map/all_to_all | solution.py:320
  105.5 0.0 collective-permute-done.6
  105.5 0.0 collective-permute-done.5
  105.5 0.0 collective-permute-done.4
  105.6 1.7 %fusion = (bf16[128,1024]{1,0:T(8,128)(2,1)S(1)}, f32[128,1024]{1,0:T(8,128)S(1)}) fusion(bf16[2,128,1024]{2,1,0:T(8,128)(2,1)S(1)} %get-tuple-element.41, bf16[2,128,1024]{2,1,0:T(8,128)(2,1)} %collective-permute-done.6, bf16[2,128,1024]{2,1,0:T(8,128)(2,1)} %collective-permute-done.5, bf16[2,128,1024]{2,1,0:T(8,128)(2,1)} %collective-permute-done.4), kind=kLoop, calls=%fused_computation.2 | loop fusion | flops 1966080 | bytes 2883584 | tf_op jit(solution)/shard_map/add | solution.py:417
  107.3 2.6 %collective-permute-start.7 = (bf16[128,1024]{1,0:T(8,128)(2,1)S(1)}, bf16[128,1024]{1,0:T(8,128)(2,1)S(1)}, u32[]{:S(2)}, u32[]{:S(2)}) collective-permute-start(bf16[128,1024]{1,0:T(8,128)(2,1)S(1)} %get-tuple-element.47), channel_id=1, source_target_pairs={{0,1},{1,0},{2,3},{3,2},{4,5},{5,4},{6,7},{7,6},{8,9},{9,8},{10,11... | collective-permute-start | bytes 786440 | tf_op jit(solution)/shard_map/ppermute | solution.py:421
  109.9 4.7 %collective-permute-done.8.shared_hbm = bf16[16,192,128]{2,1,0:T(8,128)(2,1)} collective-permute-done((bf16[16,192,128]{2,1,0:T(8,128)(2,1)}, bf16[16,192,128]{2,1,0:T(8,128)(2,1)}, u32[]{:S(2)}, u32[]{:S(2)}) %collective-permute-start.8) | collective-permute-done | bytes 786464 | tf_op jit(solution)/shard_map/ppermute | solution.py:403
  114.6 0.0 all-gather.4.cloned.1.call-done
  114.6 6.3 %weight_grad.1 = bf16[1024,512]{1,0:T(8,128)(2,1)} custom-call(s32[2]{0:T(128)} %copy-done.5, bf16[4,512,1024]{2,1,0:T(8,128)(2,1)} %bitcast.9, bf16[16,384,128]{2,1,0:T(8,128)(2,1)} %copy-done, bf16[16,192,128]{2,1,0:T(8,128)(2,1)} %collective-permute-done.8.shared_hbm), custom_call_target="tpu_custom_call" | custom-call | bytes 21000000 | tf_op jit(solution)/shard_map/weight_grad/pallas_call | solution.py:423
  120.9 0.0 all-to-all-done.3.recv_ref
  120.9 1.1 finish.1
  122.0 0.0 collective-permute-done.7.other_ref
  122.0 0.7 add_opposite.1
Async XLA Ops:
  7.2 39.2 %all-gather.6.cloned.1.call-start = ((), (), s32[]{:S(2)}) async-start(), calls=%async_computation.5 | async-start | bytes 1310720 | tf_op jit(solution)/shard_map/all_gather | solution.py:354
  7.9 9.8 %collective-permute-start = (bf16[128,1024]{1,0:T(8,128)(2,1)}, bf16[128,1024]{1,0:T(8,128)(2,1)S(1)}, u32[]{:S(2)}, u32[]{:S(2)}) collective-permute-start(bf16[128,1024]{1,0:T(8,128)(2,1)} %param.10), channel_id=1, source_target_pairs={{0,1},{1,0},{2,3},{3,2},{4,5},{5,4},{6,7},{7,6},{8,9},{9,8},{10,11... | collective-permute-start | bytes 786440 | tf_op jit(solution)/shard_map/ppermute | solution.py:346
  13.9 32.5 %copy-start.3 = (bf16[128,1024]{1,0:T(8,128)(2,1)S(1)}, bf16[128,1024]{1,0:T(8,128)(2,1)}, u32[]{:S(2)}) copy-start(bf16[128,1024]{1,0:T(8,128)(2,1)} %gate_ref.3) | copy-start | bytes 786436
  17.7 16.8 %all-to-all-start = ((bf16[16,128,128]{2,1,0:T(8,128)(2,1)}), bf16[16,128,128]{2,1,0:T(8,128)(2,1)S(1)}, u32[]{:S(2)}, u32[]{:S(2)}) async-start(bf16[16,128,128]{2,1,0:T(8,128)(2,1)} %pack.1), calls=%async_computation | async-start | bytes 1048576 | tf_op jit(solution)/shard_map/all_to_all | solution.py:320
  24.6 19.9 %collective-permute-start.1 = (bf16[128,1024]{1,0:T(8,128)(2,1)S(1)}, bf16[128,1024]{1,0:T(8,128)(2,1)S(1)}, u32[]{:S(2)}, u32[]{:S(2)}) collective-permute-start(bf16[128,1024]{1,0:T(8,128)(2,1)S(1)} %collective-permute-done.far0_ref), channel_id=1, source_target_pairs={{0,2},{1,3},{2,4},{3,5},{4,6},{5,7},{6,0},{7,1},{8,10},{9,11},{10,... | collective-permute-start | bytes 786440 | tf_op jit(solution)/shard_map/ppermute | solution.py:356
  26.2 20.2 %collective-permute-start.2 = (bf16[128,1024]{1,0:T(8,128)(2,1)S(1)}, bf16[128,1024]{1,0:T(8,128)(2,1)S(1)}, u32[]{:S(2)}, u32[]{:S(2)}) collective-permute-start(bf16[128,1024]{1,0:T(8,128)(2,1)S(1)} %collective-permute-done.far0_ref), channel_id=1, source_target_pairs={{0,4},{1,5},{2,6},{3,7},{4,0},{5,1},{6,2},{7,3},{8,12},{9,13},{10,... | collective-permute-start | bytes 786440 | tf_op jit(solution)/shard_map/ppermute | solution.py:356
  29.5 16.9 %collective-permute-start.3 = (bf16[128,1024]{1,0:T(8,128)(2,1)S(1)}, bf16[128,1024]{1,0:T(8,128)(2,1)S(1)}, u32[]{:S(2)}, u32[]{:S(2)}) collective-permute-start(bf16[128,1024]{1,0:T(8,128)(2,1)S(1)} %collective-permute-done.far0_ref), channel_id=1, source_target_pairs={{0,6},{1,7},{2,0},{3,1},{4,2},{5,3},{6,4},{7,5},{8,14},{9,15},{10,... | collective-permute-start | bytes 786440 | tf_op jit(solution)/shard_map/ppermute | solution.py:356
  34.5 1.8 %copy-start.1 = (bf16[42,256,128]{2,1,0:T(8,128)(2,1)S(1)}, bf16[42,256,128]{2,1,0:T(8,128)(2,1)}, u32[]{:S(2)}) copy-start(bf16[42,256,128]{2,1,0:T(8,128)(2,1)} %constant.30.clone.table_ref) | copy-start | bytes 8257540
  39.9 17.1 %all-to-all-start.1 = ((bf16[16,64,128]{2,1,0:T(8,128)(2,1)}), bf16[16,64,128]{2,1,0:T(8,128)(2,1)S(1)}, u32[]{:S(2)}, u32[]{:S(2)}) async-start(bf16[16,64,128]{2,1,0:T(8,128)(2,1)} %get-tuple-element.27), calls=%async_computation.1 | async-start | bytes 524288 | tf_op jit(solution)/shard_map/all_to_all | solution.py:320
  44.3 70.4 %all-gather.4.cloned.1.call-start = ((), (), s32[]{:S(2)}) async-start(), calls=%async_computation.4 | async-start | bytes 4456448 | tf_op jit(solution)/shard_map/all_gather | solution.py:387
  44.4 19.5 %copy-start.5 = (s32[2]{0:T(128)}, s32[2]{0:T(128)S(1)}, u32[]{:S(2)}) copy-start(s32[2]{0:T(128)S(1)} %pad_add_fusion.spot_ref) | copy-start | bytes 28
  46.4 1.2 copy-start.4
  58.0 34.6 %all-to-all-start.2 = ((bf16[16,384,128]{2,1,0:T(8,128)(2,1)}), bf16[16,384,128]{2,1,0:T(8,128)(2,1)S(1)}, u32[]{:S(2)}, u32[]{:S(2)}) async-start(bf16[16,384,128]{2,1,0:T(8,128)(2,1)} %get-tuple-element.32), calls=%async_computation.2 | async-start | bytes 3145728 | tf_op jit(solution)/shard_map/all_to_all | solution.py:320
  72.5 33.1 %collective-permute-start.6 = (bf16[2,128,1024]{2,1,0:T(8,128)(2,1)}, bf16[2,128,1024]{2,1,0:T(8,128)(2,1)}, u32[]{:S(2)}, u32[]{:S(2)}) collective-permute-start(bf16[2,128,1024]{2,1,0:T(8,128)(2,1)} %get-tuple-element.38), channel_id=1, source_target_pairs={{0,6},{1,7},{2,0},{3,1},{4,2},{5,3},{6,4},{7,5},{8,14},{9,15},{10,... | collective-permute-start | bytes 1572872 | tf_op jit(solution)/shard_map/ppermute | solution.py:400
  74.7 30.8 %collective-permute-start.5 = (bf16[2,128,1024]{2,1,0:T(8,128)(2,1)}, bf16[2,128,1024]{2,1,0:T(8,128)(2,1)}, u32[]{:S(2)}, u32[]{:S(2)}) collective-permute-start(bf16[2,128,1024]{2,1,0:T(8,128)(2,1)} %get-tuple-element.36), channel_id=1, source_target_pairs={{0,2},{1,3},{2,4},{3,5},{4,6},{5,7},{6,0},{7,1},{8,10},{9,11},{10,... | collective-permute-start | bytes 1572872 | tf_op jit(solution)/shard_map/ppermute | solution.py:400
  74.7 30.8 %collective-permute-start.4 = (bf16[2,128,1024]{2,1,0:T(8,128)(2,1)}, bf16[2,128,1024]{2,1,0:T(8,128)(2,1)}, u32[]{:S(2)}, u32[]{:S(2)}) collective-permute-start(bf16[2,128,1024]{2,1,0:T(8,128)(2,1)} %get-tuple-element.31), channel_id=1, source_target_pairs={{0,4},{1,5},{2,6},{3,7},{4,0},{5,1},{6,2},{7,3},{8,12},{9,13},{10,... | collective-permute-start | bytes 1572872 | tf_op jit(solution)/shard_map/ppermute | solution.py:400
  92.6 7.4 %copy-start = (bf16[16,384,128]{2,1,0:T(8,128)(2,1)}, bf16[16,384,128]{2,1,0:T(8,128)(2,1)S(1)}, u32[]{:S(2)}) copy-start(bf16[16,384,128]{2,1,0:T(8,128)(2,1)S(1)} %all-to-all-done.2.grad_ref.received_hbm) | copy-start | bytes 4718596
  93.7 21.0 %collective-permute-start.8 = (bf16[16,192,128]{2,1,0:T(8,128)(2,1)}, bf16[16,192,128]{2,1,0:T(8,128)(2,1)}, u32[]{:S(2)}, u32[]{:S(2)}) collective-permute-start(bf16[16,192,128]{2,1,0:T(8,128)(2,1)} %slice.36), channel_id=1, source_target_pairs={{0,2},{1,3},{2,0},{3,1},{4,6},{5,7},{6,4},{7,5},{8,10},{9,11},{10,... | collective-permute-start | bytes 2359304 | tf_op jit(solution)/shard_map/ppermute | solution.py:403
  94.3 1.8 %copy-start.2 = (bf16[42,256,128]{2,1,0:T(8,128)(2,1)S(1)}, bf16[42,256,128]{2,1,0:T(8,128)(2,1)}, u32[]{:S(2)}) copy-start(bf16[42,256,128]{2,1,0:T(8,128)(2,1)} %constant.30.clone.table_ref) | copy-start | bytes 8257540
  100.0 20.9 %all-to-all-start.3 = ((bf16[16,128,128]{2,1,0:T(8,128)(2,1)}), bf16[16,128,128]{2,1,0:T(8,128)(2,1)S(1)}, u32[]{:S(2)}, u32[]{:S(2)}) async-start(bf16[16,128,128]{2,1,0:T(8,128)(2,1)} %correlate.1), calls=%async_computation.3 | async-start | bytes 1048576 | tf_op jit(solution)/shard_map/all_to_all | solution.py:320
  107.3 14.8 %collective-permute-start.7 = (bf16[128,1024]{1,0:T(8,128)(2,1)S(1)}, bf16[128,1024]{1,0:T(8,128)(2,1)S(1)}, u32[]{:S(2)}, u32[]{:S(2)}) collective-permute-start(bf16[128,1024]{1,0:T(8,128)(2,1)S(1)} %get-tuple-element.47), channel_id=1, source_target_pairs={{0,1},{1,0},{2,3},{3,2},{4,5},{5,4},{6,7},{7,6},{8,9},{9,8},{10,11... | collective-permute-start | bytes 786440 | tf_op jit(solution)/shard_map/ppermute | solution.py:421
Sparse Core Ops, SparseCore 0:
  9.7 33.3 all-gather.5
  58.2 50.5 all-gather.3
